TPU v7x, 256 devices: a whole 4x4x8 slice. The times are simulated.
256 devices in a mesh: dp: 64 (over z, x, core), layer: 4 (over y).
Axes of the slice: x: 4, y: 4, z: 8, core: 2. Of those that a mesh axis runs over, the one named last changes fastest.
Arguments:
- output_grad: bfloat16 [4, 64, 128, 7168], P('layer', None, 'dp')
- output_momentum: float32 [4, 64, 128, 7168], P('layer', None, 'dp'), may hold values from -3 to 3
- values_grad: bfloat16 [4, 64, 256, 512], P('layer', None, 'dp')
- values_momentum: float32 [4, 64, 256, 512], P('layer', None, 'dp'), may hold values from -3 to 3
- owner_table: int32 [4, 2, 64, 1], P('layer'), may hold values from 0 to 63; in each aligned block of 64 rows (0 to 63, 64 to 127, ..., all dimensions but the last counted through in order) at most 3 rows name the same one
Outputs:
- output_update: bfloat16 [4, 64, 128, 7168], P('layer', None, 'dp')
- output_next: float32 [4, 64, 128, 7168], P('layer', None, 'dp')
- values_update: bfloat16 [4, 64, 256, 512], P('layer', None, 'dp')
- values_next: float32 [4, 64, 256, 512], P('layer', None, 'dp')
- slot_rms: float32 [4, 2, 64, 3], P('layer', None, 'dp')
Inputs may be any that keep to these rules, and one draw needn't show every extreme that they name: `owner_table`: for each layer and kind, no owner is named for more than 3 heads, and in some layer and kind one owner is named for exactly 3.
All inputs are finite; a program needn't handle non-finite values.
Results may differ from a plain program's by a relative error of at most 0.012.
Values may be sent and summed in bfloat16 or wider, within the bound.
No kernel may reach another device: no remote copies, remote signals or barrier semaphores. Data moves between devices by JAX's collectives and lax.ppermute only.
A program may use at most 128 MiB of HBM per device.

v0:
```python
import functools
import math

import jax
import jax.numpy as jnp
from jax import lax
from jax.experimental import pallas as pl
from jax.experimental.pallas import tpu as pltpu
from jax.sharding import PartitionSpec as P

MOMENT = 0.95
COEF_A = 3.4445
COEF_B = -4.775
COEF_C = 2.0315
CLIP_RMS = 0.5
LANES = 128
F32 = jnp.float32
BF16 = jnp.bfloat16


def flat(x):
    heads, rows, columns = x.shape
    x = x.reshape(heads, rows, columns // LANES, LANES).transpose(0, 2, 1, 3)
    return x.reshape(heads, rows * columns // LANES, LANES)


def unflat(x, rows):
    heads, depth, _ = x.shape
    x = x.reshape(heads, depth // rows, rows, LANES).transpose(0, 2, 1, 3)
    return x.reshape(heads, rows, depth // rows * LANES)


def squares_kernel(out_ref, val_ref, sum_ref):
    total = jnp.zeros((8, LANES), F32)
    for ref in (out_ref, val_ref):
        wide = ref[...].astype(F32).reshape(-1, 8, LANES)
        total = total + jnp.sum(wide * wide, axis=0)
    sum_ref[...] = jnp.broadcast_to(jnp.sum(total, axis=0, keepdims=True), sum_ref.shape)


def local_squares(out_grad, val_grad, pieces):
    vmem = pl.BlockSpec(memory_space=pltpu.VMEM)
    return pl.pallas_call(
        squares_kernel,
        in_specs=[vmem, vmem],
        out_specs=vmem,
        out_shape=jax.ShapeDtypeStruct((pieces, LANES), F32),
        compiler_params=pltpu.CompilerParams(vmem_limit_bytes=16 * 1024 * 1024),
        name="squares",
    )(out_grad, val_grad)


def prepare_kernel(om_ref, vm_ref, decayed_ref):
    depth = om_ref.shape[1]
    decayed_ref[:, :depth, :] = (MOMENT * MOMENT) * om_ref[...]
    decayed_ref[:, depth:, :] = (MOMENT * MOMENT) * vm_ref[...]


def prepare(out_momentum, val_momentum):
    heads = out_momentum.shape[0]
    depth = out_momentum.shape[1] + val_momentum.shape[1]
    vmem = pl.BlockSpec(memory_space=pltpu.VMEM)
    return pl.pallas_call(
        prepare_kernel,
        in_specs=[vmem, vmem],
        out_specs=vmem,
        out_shape=jax.ShapeDtypeStruct((heads, depth, LANES), F32),
        compiler_params=pltpu.CompilerParams(vmem_limit_bytes=16 * 1024 * 1024),
        name="prepare",
    )(out_momentum, val_momentum)


def clip_of(parts, count):
    total = jnp.sum(jnp.sum(parts, axis=0, keepdims=True), axis=1, keepdims=True)
    return jnp.minimum(1.0, CLIP_RMS * math.sqrt(count) / jnp.sqrt(total + 1e-06))


def send_kernel(count, parts_ref, og_ref, vg_ref, decayed_ref, send_ref, clip_ref):
    clip = jnp.broadcast_to(clip_of(parts_ref[...], count), clip_ref.shape)
    clip_ref[...] = clip
    factor = ((1.0 + MOMENT) * clip[0:1]).reshape(1, 1, LANES)
    depth = og_ref.shape[1]
    send_ref[:, :depth, :] = (factor * og_ref[...].astype(F32) + decayed_ref[:, :depth, :]).astype(BF16)
    send_ref[:, depth:, :] = (factor * vg_ref[...].astype(F32) + decayed_ref[:, depth:, :]).astype(BF16)


def rows_to_send(parts, count, out_grad, val_grad, decayed):
    vmem = pl.BlockSpec(memory_space=pltpu.VMEM)
    return pl.pallas_call(
        functools.partial(send_kernel, count),
        in_specs=[vmem] * 4,
        out_specs=[vmem, vmem],
        out_shape=[jax.ShapeDtypeStruct(decayed.shape, BF16), jax.ShapeDtypeStruct((8, LANES), F32)],
        compiler_params=pltpu.CompilerParams(vmem_limit_bytes=24 * 1024 * 1024),
        name="send",
    )(parts, out_grad, val_grad, decayed)


def next_kernel(clip_ref, og_ref, om_ref, vg_ref, vm_ref, on_ref, vn_ref):
    clip = clip_ref[0:1, :].reshape(1, 1, LANES)
    on_ref[...] = MOMENT * om_ref[...] + clip * og_ref[...].astype(F32)
    vn_ref[...] = MOMENT * vm_ref[...] + clip * vg_ref[...].astype(F32)


def next_momentum(clip, out_grad, out_momentum, val_grad, val_momentum, steps=8):
    heads = out_grad.shape[0]
    block = heads // steps

    def spec(x):
        return pl.BlockSpec((block,) + x.shape[1:], lambda i: (i, 0, 0))

    return pl.pallas_call(
        next_kernel,
        grid=(steps,),
        in_specs=[pl.BlockSpec((8, LANES), lambda i: (0, 0))]
        + [spec(x) for x in (out_grad, out_momentum, val_grad, val_momentum)],
        out_specs=[spec(out_grad), spec(val_grad)],
        out_shape=[jax.ShapeDtypeStruct(x.shape, F32) for x in (out_grad, val_grad)],
        name="next",
    )(clip, out_grad, out_momentum, val_grad, val_momentum)


def dot(a, b):
    return lax.dot_general(a.astype(BF16), b.astype(BF16), (((1,), (0,)), ((), ())), preferred_element_type=F32)


def polynomial(gram):
    size = gram.shape[0]
    rows = lax.broadcasted_iota(jnp.int32, gram.shape, 0)
    columns = lax.broadcasted_iota(jnp.int32, gram.shape, 1)
    diagonal = jnp.where(rows == columns, gram, 0.0)
    squares = jnp.sum(jnp.sum(diagonal, axis=0, keepdims=True), axis=1, keepdims=True)
    scale = 1.0 / (jnp.sqrt(squares) + 1e-07)
    gram = (gram * scale) * scale
    first = COEF_B * gram + COEF_C * dot(gram, gram)
    bent = dot(first, gram)
    gram = COEF_A * COEF_A * gram + 2.0 * COEF_A * bent + dot(first, bent)
    second = COEF_B * gram + COEF_C * dot(gram, gram)
    return squares, scale, COEF_A * (first + second) + dot(second, first)


def thirds(value):
    high = value.astype(BF16).astype(F32)
    middle = (value - high).astype(BF16).astype(F32)
    low = value - high - middle
    lane = lax.broadcasted_iota(jnp.int32, (1, LANES), 1)
    return jnp.where(lane == 0, high, jnp.where(lane == 1, middle, jnp.where(lane == 2, low, 0.0)))


def orthogonal_kernel(sizes, got_ref, back_ref, wide_ref, out_ref, val_ref):
    (out_rows, out_columns), (val_rows, val_columns) = sizes
    sources = out_ref.shape[0] // out_rows
    taken, given = got_ref.shape[0] // sources, back_ref.shape[0] // sources
    pitch = wide_ref.shape[0] // sources

    def spread_out(s, _):
        wide_ref[pl.ds(pl.multiple_of(s * pitch, 8), taken), :] = got_ref[
            pl.ds(pl.multiple_of(s * taken, 16), taken), :
        ].astype(F32)
        return 0

    lax.fori_loop(0, sources, spread_out, 0, unroll=4)

    offset = 0
    for ref, rows, columns in ((out_ref, out_rows, out_columns), (val_ref, val_rows, val_columns)):
        for j in range(columns // LANES):
            parts = [
                wide_ref[pl.ds(offset + j * rows + r, sources, stride=pitch), :].astype(BF16) for r in range(rows)
            ]
            ref[:, j * LANES : (j + 1) * LANES] = jnp.concatenate(parts, axis=0)
        offset += columns // LANES * rows

    offset = 0
    spreads = []
    for ref, rows, columns in ((out_ref, out_rows, out_columns), (val_ref, val_rows, val_columns)):
        whole = ref[...]
        gram = lax.dot_general(whole, whole, (((1,), (1,)), ((), ())), preferred_element_type=F32)
        squares, scale, factor = polynomial(gram)
        factor = factor.astype(BF16)
        height = rows * sources
        final = scale * math.sqrt(max(height, columns))
        spreads.append(jnp.sqrt(squares / (height * columns)))
        width = 512
        for at in range(columns // width):
            piece = ref[:, at * width : (at + 1) * width]
            product = lax.dot_general(factor, piece, (((1,), (0,)), ((), ())), preferred_element_type=F32)
            product = final * (COEF_A * COEF_A * piece.astype(F32) + product)
            for k in range(width // LANES):
                j = at * (width // LANES) + k
                for r in range(rows):
                    wide_ref[pl.ds(offset + j * rows + r, sources, stride=given), :] = product[
                        r * sources : (r + 1) * sources, k * LANES : (k + 1) * LANES
                    ]
        offset += columns // LANES * rows
    for r, spread in enumerate(spreads):
        wide_ref[pl.ds(offset + r, sources, stride=given), :] = jnp.broadcast_to(thirds(spread), (sources, LANES))

    chunk = given * 8

    def gather(i, _):
        rows = pl.ds(pl.multiple_of(i * chunk, 16), chunk)
        back_ref[rows, :] = wide_ref[rows, :].astype(BF16)
        return 0

    lax.fori_loop(0, sources // 8, gather, 0)


def orthogonalize(got, sizes, sources, given, pitch=136):
    (out_rows, out_columns), (val_rows, val_columns) = sizes
    return pl.pallas_call(
        functools.partial(orthogonal_kernel, sizes),
        out_shape=jax.ShapeDtypeStruct((sources * given, LANES), BF16),
        scratch_shapes=[
            pltpu.VMEM((sources * pitch, LANES), F32),
            pltpu.VMEM((out_rows * sources, out_columns), BF16),
            pltpu.VMEM((val_rows * sources, val_columns), BF16),
        ],
        compiler_params=pltpu.CompilerParams(vmem_limit_bytes=40 * 1024 * 1024),
        name="orthogonal",
    )(got)


def finish_kernel(given, back_ref, choice_ref, out_ref, val_ref, slot_ref):
    @pl.when(pl.program_id(0) == 0)
    def _():
        slot_ref[...] = jnp.zeros_like(slot_ref)

    block, out_depth, _ = out_ref.shape
    val_depth = val_ref.shape[1]
    total = jnp.zeros(slot_ref.shape, F32)
    for p in range(block):
        start = p * given
        out_ref[p] = back_ref[start : start + out_depth, :]
        start += out_depth
        val_ref[p] = back_ref[start : start + val_depth, :]
        start += val_depth
        spread = jnp.sum(back_ref[start : start + 2, :].astype(F32), axis=1, keepdims=True)
        total = total + spread * choice_ref[p]
    slot_ref[...] += total


def finish(back, choice, out_depth, val_depth, given, steps=8):
    heads = choice.shape[0]
    block = heads // steps

    def spec(depth):
        return pl.BlockSpec((block, depth, LANES), lambda i: (i, 0, 0))

    return pl.pallas_call(
        functools.partial(finish_kernel, given),
        grid=(steps,),
        in_specs=[pl.BlockSpec((block * given, LANES), lambda i: (i, 0)), spec(2)],
        out_specs=[spec(out_depth), spec(val_depth), pl.BlockSpec((2, LANES), lambda i: (0, 0))],
        out_shape=[
            jax.ShapeDtypeStruct((heads, out_depth, LANES), BF16),
            jax.ShapeDtypeStruct((heads, val_depth, LANES), BF16),
            jax.ShapeDtypeStruct((2, LANES), F32),
        ],
        name="finish",
    )(back, choice)


def slot_choice(table, owner):
    mine = (table == owner).astype(jnp.int32)
    heads = mine.shape[1]
    index = lax.iota(jnp.int32, heads)
    earlier = (index[None, :] < index[:, None]).astype(jnp.int32)
    rank = jnp.sum(earlier[None] * mine[:, None, :], axis=2)
    lane = lax.iota(jnp.int32, LANES)
    chosen = (mine[:, :, None] == 1) & (rank[:, :, None] == lane[None, None, :])
    return chosen.astype(F32).transpose(1, 0, 2)


def body(output_grad, output_momentum, values_grad, values_momentum, owner_table):
    owners, layers = lax.axis_size("dp"), lax.axis_size("layer")
    out_rows, out_columns = output_grad.shape[2:]
    val_rows, val_columns = values_grad.shape[2:]
    capacity = 3
    out_grad, out_momentum = flat(output_grad[0]), flat(output_momentum[0])
    val_grad, val_momentum = flat(values_grad[0]), flat(values_momentum[0])
    heads = out_grad.shape[0]

    everyone = owners * layers
    parts = lax.all_to_all(
        local_squares(out_grad, val_grad, everyone).reshape(everyone, 1, LANES),
        ("dp", "layer"),
        split_axis=0,
        concat_axis=0,
        tiled=True,
    ).reshape(everyone, LANES)
    count = (output_grad.size + values_grad.size) * everyone

    decayed = prepare(out_momentum, val_momentum)
    send, clip = rows_to_send(parts, count, out_grad, val_grad, decayed)
    out_next, val_next = next_momentum(clip, out_grad, out_momentum, val_grad, val_momentum)
    got = lax.all_to_all(send, "dp", split_axis=0, concat_axis=0, tiled=True)

    out_depth, val_depth = out_grad.shape[1], val_grad.shape[1]
    given = out_depth + val_depth + 2
    back = orthogonalize(
        got.reshape(heads * (out_depth + val_depth), LANES),
        ((out_rows, out_columns), (val_rows, val_columns)),
        owners,
        given,
    )
    back = lax.all_to_all(
        back.reshape(heads, given // 2, 2, LANES), "dp", split_axis=0, concat_axis=0, tiled=True
    )
    choice = slot_choice(owner_table[0, :, :, 0], lax.axis_index("dp"))
    out_update, val_update, slots = finish(
        back.reshape(heads * given, LANES), choice, out_depth, val_depth, given
    )

    return (
        unflat(out_update.reshape(out_grad.shape), out_rows)[None],
        unflat(out_next, out_rows)[None],
        unflat(val_update.reshape(val_grad.shape), val_rows)[None],
        unflat(val_next, val_rows)[None],
        slots[None, :, None, :capacity],
    )


def solution(mesh):
    rows = P("layer", None, "dp", None)
    return jax.shard_map(
        body,
        mesh=mesh,
        in_specs=(rows, rows, rows, rows, P("layer", None, None, None)),
        out_specs=(rows, rows, rows, rows, rows),
        check_vma=False,
    )
```

profile of v0, /device:TPU:2, one launch (start us, length us, event | category | flops | bytes accessed | tf_op | source)
XLA Modules:
  0.0 161.7 jit_solution(17192779113139699815)
XLA Ops:
  0.6 0.0 copy-start.2
  0.6 1.5 copy-done.2
  2.1 0.0 copy-start.5
  2.1 0.9 copy-done.5
  3.1 0.0 copy-start.7
  3.1 1.6 squares.1
  4.7 14.7 %all-to-all-start = ((f32[256,1,128]{2,1,0:T(1,128)}), f32[256,1,128]{2,1,0:T(1,128)S(1)}, u32[]{:S(2)}, u32[]{:S(2)}) async-start(f32[256,1,128]{2,1,0:T(1,128)} %bitcast.7), calls=%async_computation | async-start | bytes 262144 | tf_op jit(solution)/shard_map/all_to_all | solution.py:284
  19.4 0.0 copy-done.7
  19.4 0.0 copy-start.4
  19.4 2.0 %copy-done.4 = f32[1,64,2,7168]{3,2,1,0:T(2,128)S(1)} copy-done((f32[1,64,2,7168]{3,2,1,0:T(2,128)S(1)}, f32[1,64,2,7168]{3,2,1,0:T(2,128)}, u32[]{:S(2)}) %copy-start.4) | copy-done | bytes 3670040
  21.5 0.0 copy-start.3
  21.5 0.0 copy-start.6
  21.5 0.4 prepare.1.decayed_ref
  21.8 0.0 copy-start
  21.8 1.9 %copy-done = f32[64,128,128]{2,1,0:T(8,128)} copy-done((f32[64,128,128]{2,1,0:T(8,128)}, f32[64,128,128]{2,1,0:T(8,128)S(1)}, u32[]{:S(2)}) %copy-start) | copy-done | bytes 4194328
  23.8 7.6 %all-to-all-done = f32[256,1,128]{2,1,0:T(1,128)S(1)} async-done(((f32[256,1,128]{2,1,0:T(1,128)}), f32[256,1,128]{2,1,0:T(1,128)S(1)}, u32[]{:S(2)}, u32[]{:S(2)}) %all-to-all-start) | async-done | bytes 131104 | tf_op jit(solution)/shard_map/all_to_all | solution.py:284
  31.3 0.0 copy-done.3
  31.3 0.0 copy-done.6
  31.3 0.0 copy-start.1
  31.3 2.2 %copy-done.1 = f32[64,128,128]{2,1,0:T(8,128)S(1)} copy-done((f32[64,128,128]{2,1,0:T(8,128)S(1)}, f32[64,128,128]{2,1,0:T(8,128)}, u32[]{:S(2)}) %copy-start.1) | copy-done | bytes 4194328
  33.5 1.3 send.1
  34.8 0.0 copy-start.8
  34.8 56.4 %all_to_all.15 = bf16[64,128,128]{2,1,0:T(8,128)(2,1)S(1)} all-to-all(bf16[64,128,128]{2,1,0:T(8,128)(2,1)S(1)} %get-tuple-element.12), channel_id=1, replica_groups=mesh['dp'=64,'layer'=4] {'dp'}, dimensions={0} | all-to-all | bytes 4194304 | tf_op jit(solution)/shard_map/all_to_all | solution.py:296
  91.2 5.7 %orthogonal.1 = bf16[8320,128]{1,0:T(8,128)(2,1)} custom-call(bf16[8192,128]{1,0:T(8,128)(2,1)S(1)} %bitcast.60), custom_call_target="tpu_custom_call" | custom-call | tf_op jit(solution)/shard_map/orthogonal/pallas_call | solution.py:210
  97.0 0.0 copy-done.8
  97.0 0.0 copy-start.10
  97.0 5.6 %all-to-all-start.2 = ((bf16[64,65,2,128]{3,2,1,0:T(2,128)(2,1)}), bf16[64,65,2,128]{3,2,1,0:T(2,128)(2,1)S(1)}, u32[]{:S(2)}, u32[]{:S(2)}) async-start(bf16[64,65,2,128]{3,2,1,0:T(2,128)(2,1)} %bitcast.16), calls=%async_computation.2 | async-start | bytes 4259840 | tf_op jit(solution)/shard_map/all_to_all | solution.py:306
  102.6 0.0 copy-done.10
  102.6 0.1 copy.36
  102.7 0.1 multiply_reduce_fusion
  102.8 0.1 copy.37
  102.9 0.8 and_convert_fusion.choice_ref
  103.8 7.0 %next.1 = (f32[64,112,128]{2,1,0:T(8,128)}, f32[64,16,128]{2,1,0:T(8,128)}) custom-call(f32[8,128]{1,0:T(8,128)} %copy-done.8, bf16[64,112,128]{2,1,0:T(8,128)(2,1)} %bitcast.55, f32[64,112,128]{2,1,0:T(8,128)} %bitcast.58, bf16[64,16,128]{2,1,0:T(8,128)(2,1)} %bitcast.61, f32[64,16,128]{2,1,0:T(8,128)} %bitcast.64), custom_call_target="tpu_custom_call" | custom-call | tf_op jit(solution)/shard_map/next/pallas_call | solution.py:112
  110.8 43.7 %all-to-all-done.2 = bf16[64,65,2,128]{3,2,1,0:T(2,128)(2,1)S(1)} async-done(((bf16[64,65,2,128]{3,2,1,0:T(2,128)(2,1)}), bf16[64,65,2,128]{3,2,1,0:T(2,128)(2,1)S(1)}, u32[]{:S(2)}, u32[]{:S(2)}) %all-to-all-start.2) | async-done | bytes 2129952 | tf_op jit(solution)/shard_map/all_to_all | solution.py:306
  154.5 0.0 copy-start.9
  154.5 1.4 copy-done.9
  155.9 5.8 %finish.1 = (bf16[64,112,128]{2,1,0:T(8,128)(2,1)}, bf16[64,16,128]{2,1,0:T(8,128)(2,1)}, f32[2,128]{1,0:T(2,128)}) custom-call(bf16[8320,128]{1,0:T(8,128)(2,1)} %bitcast.67, f32[64,2,128]{2,1,0:T(2,128)} %and_convert_fusion.choice_ref), custom_call_target="tpu_custom_call" | custom-call | tf_op jit(solution)/shard_map/finish/pallas_call | solution.py:249
  (3 shorter events, 0.0 us)
Async XLA Ops:
  0.6 1.5 copy-start.2
  2.1 0.9 copy-start.5
  3.1 16.3 %copy-start.7 = (f32[1,64,4,512]{3,2,1,0:T(4,128)S(1)}, f32[1,64,4,512]{3,2,1,0:T(4,128)}, u32[]{:S(2)}) copy-start(f32[1,64,4,512]{3,2,1,0:T(4,128)} %param.8) | copy-start | bytes 1572868
  4.7 26.6 %all-to-all-start = ((f32[256,1,128]{2,1,0:T(1,128)}), f32[256,1,128]{2,1,0:T(1,128)S(1)}, u32[]{:S(2)}, u32[]{:S(2)}) async-start(f32[256,1,128]{2,1,0:T(1,128)} %bitcast.7), calls=%async_computation | async-start | bytes 262144 | tf_op jit(solution)/shard_map/all_to_all | solution.py:284
  19.4 2.0 %copy-start.4 = (f32[1,64,2,7168]{3,2,1,0:T(2,128)S(1)}, f32[1,64,2,7168]{3,2,1,0:T(2,128)}, u32[]{:S(2)}) copy-start(f32[1,64,2,7168]{3,2,1,0:T(2,128)} %param.6) | copy-start | bytes 11010052
  21.5 9.9 %copy-start.3 = (bf16[1,64,2,7168]{3,2,1,0:T(2,128)(2,1)S(1)}, bf16[1,64,2,7168]{3,2,1,0:T(2,128)(2,1)}, u32[]{:S(2)}) copy-start(bf16[1,64,2,7168]{3,2,1,0:T(2,128)(2,1)} %param.5) | copy-start | bytes 5505028
  21.5 9.9 %copy-start.6 = (bf16[1,64,4,512]{3,2,1,0:T(4,128)(2,1)S(1)}, bf16[1,64,4,512]{3,2,1,0:T(4,128)(2,1)}, u32[]{:S(2)}) copy-start(bf16[1,64,4,512]{3,2,1,0:T(4,128)(2,1)} %param.7) | copy-start | bytes 786436
  21.8 2.0 %copy-start = (f32[64,128,128]{2,1,0:T(8,128)}, f32[64,128,128]{2,1,0:T(8,128)S(1)}, u32[]{:S(2)}) copy-start(f32[64,128,128]{2,1,0:T(8,128)S(1)} %prepare.1.decayed_ref) | copy-start | bytes 12582916
  31.3 2.2 %copy-start.1 = (f32[64,128,128]{2,1,0:T(8,128)S(1)}, f32[64,128,128]{2,1,0:T(8,128)}, u32[]{:S(2)}) copy-start(f32[64,128,128]{2,1,0:T(8,128)} %copy-done) | copy-start | bytes 12582916
  34.8 62.2 %copy-start.8 = (f32[8,128]{1,0:T(8,128)}, f32[8,128]{1,0:T(8,128)S(1)}, u32[]{:S(2)}) copy-start(f32[8,128]{1,0:T(8,128)S(1)} %get-tuple-element.14.clip_ref) | copy-start | bytes 12292
  97.0 5.6 %copy-start.10 = (s32[1,2,64,1]{2,3,1,0:T(1,128)S(1)}, s32[1,2,64,1]{2,3,1,0:T(1,128)}, u32[]{:S(2)}) copy-start(s32[1,2,64,1]{2,3,1,0:T(1,128)} %param.9) | copy-start | bytes 1540
  97.0 57.5 %all-to-all-start.2 = ((bf16[64,65,2,128]{3,2,1,0:T(2,128)(2,1)}), bf16[64,65,2,128]{3,2,1,0:T(2,128)(2,1)S(1)}, u32[]{:S(2)}, u32[]{:S(2)}) async-start(bf16[64,65,2,128]{3,2,1,0:T(2,128)(2,1)} %bitcast.16), calls=%async_computation.2 | async-start | bytes 4259840 | tf_op jit(solution)/shard_map/all_to_all | solution.py:306
  154.5 1.4 copy-start.9
where the time goes:
time: 162 us
  blocking collectives  56.4 us (35%)
  waiting for transfers between devices  51.3 us (32%)
  Pallas kernels  21.8 us (13%)
  starting transfers between devices  20.3 us (13%)
  local copies, waits for them, and re-layouts  10.2 us (6%)
    all_to_all x1, blocking collectives, body(): got = lax.all_to_all(send, 'dp', split_axis=0, concat_axis=0, tiled=True)  56.4 us
    all_to_all x1, waiting for transfers between devices, body(): lax.all_to_all(back.reshape(heads, given // 2, 2, LANES), 'dp', split_axi...  43.7 us
    all_to_all x1, starting transfers between devices, body(): lax.all_to_all(local_squares(out_grad, val_grad, everyone).reshape(everyo...  14.7 us
    unnamed x22, local copies, waits for them, and re-layouts  9.99 us
    all_to_all x1, waiting for transfers between devices, body(): lax.all_to_all(local_squares(out_grad, val_grad, everyone).reshape(everyo...  7.56 us
    pallas_call x1, Pallas kernels, next_momentum(): pl.pallas_call(next_kernel, grid=(steps,), in_specs=[pl.BlockSpec((8, LAN...  7.01 us
    pallas_call x1, Pallas kernels, finish(): pl.pallas_call(functools.partial(finish_kernel, given), grid=(steps,), in...  5.78 us
    pallas_call x1, Pallas kernels, orthogonalize(): pl.pallas_call(functools.partial(orthogonal_kernel, sizes), out_shape=jax...  5.74 us
  transfers between devices with their start and end apart: 2, of which 2 were waited for; matrix products, arithmetic and copies ran while one was open for 1% of the time, Pallas kernels for 5%

commit v1 on v0

v1 whole, which is shorter than its diff:
```python
import functools
import math

import jax
import jax.numpy as jnp
from jax import lax
from jax.experimental import pallas as pl
from jax.experimental.pallas import tpu as pltpu
from jax.sharding import PartitionSpec as P

MOMENT = 0.95
COEF_A = 3.4445
COEF_B = -4.775
COEF_C = 2.0315
CLIP_RMS = 0.5
LANES = 128
F32 = jnp.float32
BF16 = jnp.bfloat16


def flat(x):
    heads, rows, columns = x.shape
    x = x.reshape(heads, rows, columns // LANES, LANES).transpose(0, 2, 1, 3)
    return x.reshape(heads, rows * columns // LANES, LANES)


def unflat(x, rows):
    heads, depth, _ = x.shape
    x = x.reshape(heads, depth // rows, rows, LANES).transpose(0, 2, 1, 3)
    return x.reshape(heads, rows, depth // rows * LANES)


HBM = pl.BlockSpec(memory_space=pltpu.HBM)
VMEM = pl.BlockSpec(memory_space=pltpu.VMEM)
CHUNKS = 8
GRANT = 60 * 1024 * 1024
ORTHO = 40 * 1024 * 1024


def chunk_of(ref, i):
    block = ref.shape[0] // CHUNKS
    return ref.at[pl.ds(i * block, block)]


def loads(pairs, sems):
    copies = []
    for i in range(CHUNKS):
        row = []
        for n, (source, target) in enumerate(pairs):
            copy = pltpu.make_async_copy(chunk_of(source, i), chunk_of(target, i), sems.at[n, i])
            copy.start()
            row.append(copy)
        copies.append(row)
    return copies


def squares_kernel(out_hbm, val_hbm, sum_ref, out_ref, val_ref, sems):
    copies = loads([(out_hbm, out_ref), (val_hbm, val_ref)], sems)
    total = jnp.zeros((8, LANES), F32)
    for i, row in enumerate(copies):
        for copy, ref in zip(row, (out_ref, val_ref)):
            copy.wait()
            wide = chunk_of(ref, i)[...].astype(F32).reshape(-1, 8, LANES)
            total = total + jnp.sum(wide * wide, axis=0)
    sum_ref[...] = jnp.broadcast_to(jnp.sum(total, axis=0, keepdims=True), sum_ref.shape)


def local_squares(out_grad, val_grad, pieces):
    return pl.pallas_call(
        squares_kernel,
        in_specs=[HBM, HBM],
        out_specs=VMEM,
        out_shape=jax.ShapeDtypeStruct((pieces, LANES), F32),
        scratch_shapes=[
            pltpu.VMEM(out_grad.shape, BF16),
            pltpu.VMEM(val_grad.shape, BF16),
            pltpu.SemaphoreType.DMA((2, CHUNKS)),
        ],
        compiler_params=pltpu.CompilerParams(vmem_limit_bytes=GRANT),
        name="squares",
    )(out_grad, val_grad)


def prepare_kernel(om_ref, vm_ref, decayed_ref):
    depth = om_ref.shape[1]
    decayed_ref[:, :depth, :] = (MOMENT * MOMENT) * om_ref[...]
    decayed_ref[:, depth:, :] = (MOMENT * MOMENT) * vm_ref[...]


def prepare(out_momentum, val_momentum):
    heads = out_momentum.shape[0]
    depth = out_momentum.shape[1] + val_momentum.shape[1]
    return pl.pallas_call(
        prepare_kernel,
        in_specs=[VMEM, VMEM],
        out_specs=VMEM,
        out_shape=jax.ShapeDtypeStruct((heads, depth, LANES), F32),
        compiler_params=pltpu.CompilerParams(vmem_limit_bytes=16 * 1024 * 1024),
        name="prepare",
    )(out_momentum, val_momentum)


def clip_of(parts, count):
    total = jnp.sum(jnp.sum(parts, axis=0, keepdims=True), axis=1, keepdims=True)
    return jnp.minimum(1.0, CLIP_RMS * math.sqrt(count) / jnp.sqrt(total + 1e-06))


def send_kernel(count, parts_ref, og_ref, vg_ref, decayed_ref, send_ref, clip_ref):
    clip = jnp.broadcast_to(clip_of(parts_ref[...], count), clip_ref.shape)
    clip_ref[...] = clip
    factor = ((1.0 + MOMENT) * clip[0:1]).reshape(1, 1, LANES)
    depth = og_ref.shape[1]
    send_ref[:, :depth, :] = (factor * og_ref[...].astype(F32) + decayed_ref[:, :depth, :]).astype(BF16)
    send_ref[:, depth:, :] = (factor * vg_ref[...].astype(F32) + decayed_ref[:, depth:, :]).astype(BF16)


def rows_to_send(parts, count, out_grad, val_grad, decayed):
    return pl.pallas_call(
        functools.partial(send_kernel, count),
        in_specs=[VMEM] * 4,
        out_specs=[VMEM, VMEM],
        out_shape=[jax.ShapeDtypeStruct(decayed.shape, BF16), jax.ShapeDtypeStruct((8, LANES), F32)],
        compiler_params=pltpu.CompilerParams(vmem_limit_bytes=24 * 1024 * 1024),
        name="send",
    )(parts, out_grad, val_grad, decayed)


def next_kernel(clip_ref, og_ref, om_ref, vg_ref, vm_ref, on_ref, vn_ref):
    clip = clip_ref[0:1, :].reshape(1, 1, LANES)
    on_ref[...] = MOMENT * om_ref[...] + clip * og_ref[...].astype(F32)
    vn_ref[...] = MOMENT * vm_ref[...] + clip * vg_ref[...].astype(F32)


def next_momentum(clip, out_grad, out_momentum, val_grad, val_momentum, steps=8):
    heads = out_grad.shape[0]
    block = heads // steps

    def spec(x):
        return pl.BlockSpec((block,) + x.shape[1:], lambda i: (i, 0, 0))

    return pl.pallas_call(
        next_kernel,
        grid=(steps,),
        in_specs=[pl.BlockSpec((8, LANES), lambda i: (0, 0))]
        + [spec(x) for x in (out_grad, out_momentum, val_grad, val_momentum)],
        out_specs=[spec(out_grad), spec(val_grad)],
        out_shape=[jax.ShapeDtypeStruct(x.shape, F32) for x in (out_grad, val_grad)],
        name="next",
    )(clip, out_grad, out_momentum, val_grad, val_momentum)


def dot(a, b):
    return lax.dot_general(a.astype(BF16), b.astype(BF16), (((1,), (0,)), ((), ())), preferred_element_type=F32)


def polynomials(grams):
    every, scales = [], []
    for gram in grams:
        rows = lax.broadcasted_iota(jnp.int32, gram.shape, 0)
        columns = lax.broadcasted_iota(jnp.int32, gram.shape, 1)
        diagonal = jnp.where(rows == columns, gram, 0.0)
        squares = jnp.sum(jnp.sum(diagonal, axis=0, keepdims=True), axis=1, keepdims=True)
        every.append(squares)
        scales.append(1.0 / (jnp.sqrt(squares) + 1e-07))
    grams = [(gram * scale) * scale for gram, scale in zip(grams, scales)]
    first = [COEF_B * gram + COEF_C * dot(gram, gram) for gram in grams]
    bent = [dot(f, gram) for f, gram in zip(first, grams)]
    grams = [
        COEF_A * COEF_A * gram + 2.0 * COEF_A * b + dot(f, b) for f, gram, b in zip(first, grams, bent)
    ]
    second = [COEF_B * gram + COEF_C * dot(gram, gram) for gram in grams]
    return every, scales, [COEF_A * (f + g) + dot(g, f) for f, g in zip(first, second)]


def thirds(value):
    high = value.astype(BF16).astype(F32)
    middle = (value - high).astype(BF16).astype(F32)
    low = value - high - middle
    lane = lax.broadcasted_iota(jnp.int32, (1, LANES), 1)
    return jnp.where(lane == 0, high, jnp.where(lane == 1, middle, jnp.where(lane == 2, low, 0.0)))


def orthogonal_kernel(sizes, got_ref, back_hbm, wide_ref, back_ref, out_ref, val_ref, sems):
    sources, depth, _ = got_ref.shape
    pitch, given = wide_ref.shape[0] // sources, back_ref.shape[0] // sources
    matrices = [(ref, rows, columns) for ref, (rows, columns) in zip((out_ref, val_ref), sizes)]
    for s in range(sources):
        wide_ref[s * pitch : s * pitch + depth, :] = got_ref[s].astype(F32)

    offset = 0
    grams = []
    for ref, rows, columns in matrices:
        for j in range(columns // LANES):
            parts = [
                wide_ref[pl.ds(offset + j * rows + r, sources, stride=pitch), :].astype(BF16) for r in range(rows)
            ]
            ref[:, j * LANES : (j + 1) * LANES] = jnp.concatenate(parts, axis=0)
        offset += columns // LANES * rows
        whole = ref[...]
        grams.append(lax.dot_general(whole, whole, (((1,), (1,)), ((), ())), preferred_element_type=F32))
    squares, scales, factors = polynomials(grams)

    offset = 0
    for (ref, rows, columns), scale, factor in zip(matrices, scales, factors):
        factor = factor.astype(BF16)
        final = scale * math.sqrt(max(rows * sources, columns))
        width = 512
        for at in range(0, columns, width):
            piece = ref[:, at : at + width]
            product = lax.dot_general(factor, piece, (((1,), (0,)), ((), ())), preferred_element_type=F32)
            product = final * (COEF_A * COEF_A * piece.astype(F32) + product)
            for k in range(width // LANES):
                j = at // LANES + k
                for r in range(rows):
                    wide_ref[pl.ds(offset + j * rows + r, sources, stride=given), :] = product[
                        r * sources : (r + 1) * sources, k * LANES : (k + 1) * LANES
                    ]
        offset += columns // LANES * rows

    for r, ((_, rows, columns), square) in enumerate(zip(matrices, squares)):
        spread = jnp.sqrt(square / (rows * sources * columns))
        wide_ref[pl.ds(offset + r, sources, stride=given), :] = jnp.broadcast_to(thirds(spread), (sources, LANES))

    copies = []
    for i in range(CHUNKS):
        block = back_ref.shape[0] // CHUNKS
        back_ref[i * block : (i + 1) * block, :] = wide_ref[i * block : (i + 1) * block, :].astype(BF16)
        copy = pltpu.make_async_copy(chunk_of(back_ref, i), chunk_of(back_hbm, i), sems.at[i])
        copy.start()
        copies.append(copy)
    for copy in copies:
        copy.wait()


def orthogonalize(got, sizes, given, pitch=136):
    sources = got.shape[0]
    return pl.pallas_call(
        functools.partial(orthogonal_kernel, sizes),
        in_specs=[VMEM],
        out_specs=HBM,
        out_shape=jax.ShapeDtypeStruct((sources * given, LANES), BF16),
        scratch_shapes=[pltpu.VMEM((sources * pitch, LANES), F32), pltpu.VMEM((sources * given, LANES), BF16)]
        + [pltpu.VMEM((rows * sources, columns), BF16) for rows, columns in sizes]
        + [pltpu.SemaphoreType.DMA((CHUNKS,))],
        compiler_params=pltpu.CompilerParams(vmem_limit_bytes=ORTHO),
        name="orthogonal",
    )(got)


def finish_kernel(given, back_ref, choice_ref, out_hbm, val_hbm, slot_ref, wide_ref, out_ref, val_ref, sems):
    heads, out_depth, _ = out_ref.shape
    val_depth = val_ref.shape[1]
    block = heads // CHUNKS
    total = jnp.zeros(slot_ref.shape, F32)
    copies = []
    for i in range(CHUNKS):
        span = pl.ds(i * block * given, block * given)
        wide_ref[span, :] = back_ref[span, :].astype(F32)
        for p in range(i * block, (i + 1) * block):
            start = p * given
            out_ref[p] = wide_ref[start : start + out_depth, :].astype(BF16)
            start += out_depth
            val_ref[p] = wide_ref[start : start + val_depth, :].astype(BF16)
            start += val_depth
            spread = jnp.sum(wide_ref[start : start + 2, :], axis=1, keepdims=True)
            total = total + spread * choice_ref[p]
        for n, (ref, target) in enumerate(((out_ref, out_hbm), (val_ref, val_hbm))):
            copy = pltpu.make_async_copy(chunk_of(ref, i), chunk_of(target, i), sems.at[n, i])
            copy.start()
            copies.append(copy)
    slot_ref[...] = total
    for copy in copies:
        copy.wait()


def finish(back, choice, out_depth, val_depth, given):
    heads = choice.shape[0]
    shapes = [(heads, rows, LANES) for rows in (out_depth, val_depth)]
    return pl.pallas_call(
        functools.partial(finish_kernel, given),
        in_specs=[VMEM, VMEM],
        out_specs=[HBM, HBM, VMEM],
        out_shape=[jax.ShapeDtypeStruct(shape, BF16) for shape in shapes] + [jax.ShapeDtypeStruct((2, LANES), F32)],
        scratch_shapes=[pltpu.VMEM(back.shape, F32)]
        + [pltpu.VMEM(shape, BF16) for shape in shapes]
        + [pltpu.SemaphoreType.DMA((2, CHUNKS))],
        compiler_params=pltpu.CompilerParams(vmem_limit_bytes=24 * 1024 * 1024),
        name="finish",
    )(back, choice)


def slot_choice(table, owner):
    mine = (table == owner).astype(jnp.int32)
    heads = mine.shape[1]
    index = lax.iota(jnp.int32, heads)
    earlier = (index[None, :] < index[:, None]).astype(jnp.int32)
    rank = jnp.sum(earlier[None] * mine[:, None, :], axis=2)
    lane = lax.iota(jnp.int32, LANES)
    chosen = (mine[:, :, None] == 1) & (rank[:, :, None] == lane[None, None, :])
    return chosen.astype(F32).transpose(1, 0, 2)


def body(output_grad, output_momentum, values_grad, values_momentum, owner_table):
    owners, layers = lax.axis_size("dp"), lax.axis_size("layer")
    out_rows, out_columns = output_grad.shape[2:]
    val_rows, val_columns = values_grad.shape[2:]
    capacity = 3
    out_grad, out_momentum = flat(output_grad[0]), flat(output_momentum[0])
    val_grad, val_momentum = flat(values_grad[0]), flat(values_momentum[0])
    heads = out_grad.shape[0]

    everyone = owners * layers
    parts = lax.all_to_all(
        local_squares(out_grad, val_grad, everyone).reshape(everyone, 1, LANES),
        ("dp", "layer"),
        split_axis=0,
        concat_axis=0,
        tiled=True,
    ).reshape(everyone, LANES)
    count = (output_grad.size + values_grad.size) * everyone

    decayed = prepare(out_momentum, val_momentum)
    send, clip = rows_to_send(parts, count, out_grad, val_grad, decayed)
    out_next, val_next = next_momentum(clip, out_grad, out_momentum, val_grad, val_momentum)
    got = lax.all_to_all(send, "dp", split_axis=0, concat_axis=0, tiled=True)

    out_depth, val_depth = out_grad.shape[1], val_grad.shape[1]
    given = out_depth + val_depth + 2
    back = orthogonalize(got, ((out_rows, out_columns), (val_rows, val_columns)), given)
    back = lax.all_to_all(
        back.reshape(heads, given // 2, 2, LANES), "dp", split_axis=0, concat_axis=0, tiled=True
    )
    choice = slot_choice(owner_table[0, :, :, 0], lax.axis_index("dp"))
    out_update, val_update, slots = finish(
        back.reshape(heads * given, LANES), choice, out_depth, val_depth, given
    )

    return (
        unflat(out_update.reshape(out_grad.shape), out_rows)[None],
        unflat(out_next, out_rows)[None],
        unflat(val_update.reshape(val_grad.shape), val_rows)[None],
        unflat(val_next, val_rows)[None],
        slots[None, :, None, :capacity],
    )


def solution(mesh):
    rows = P("layer", None, "dp", None)
    return jax.shard_map(
        body,
        mesh=mesh,
        in_specs=(rows, rows, rows, rows, P("layer", None, None, None)),
        out_specs=(rows, rows, rows, rows, rows),
        check_vma=False,
    )
```

time: 162 us -> 157 us (0.969)
  Pallas kernels: 21.8 us -> 18.1 us
  local copies, waits for them, and re-layouts: 10.2 us -> 8.32 us
    pallas_call x5, Pallas kernels: 14.8 us -> 11 us  [the longest x1 4.06 us: orthogonalize(): pl.pallas_call(functools.partial(orthogonal_kernel, sizes), in_specs=[VME...]
    unnamed x22 -> x18, local copies, waits for them, and re-layouts: 9.99 us -> 8.11 us
  transfers between devices with their start and end apart: 2 -> 2, of which waited for: 2 -> 2; matrix products, arithmetic and copies ran while one was open for 1% -> 0% of each run, Pallas kernels for 5% -> 5%
where the time goes in v1:
time: 157 us; the launch traced here: 156 us
  blocking collectives  56.4 us (36%)
  waiting for transfers between devices  51.9 us (33%)
  starting transfers between devices  20.3 us (13%)
  Pallas kernels  18.1 us (12%)
  local copies, waits for them, and re-layouts  8.32 us (5%)
    all_to_all x1, blocking collectives, body(): got = lax.all_to_all(send, 'dp', split_axis=0, concat_axis=0, tiled=True)  56.4 us
    all_to_all x1, waiting for transfers between devices, body(): lax.all_to_all(back.reshape(heads, given // 2, 2, LANES), 'dp', split_axi...  44.3 us
    all_to_all x1, starting transfers between devices, body(): lax.all_to_all(local_squares(out_grad, val_grad, everyone).reshape(everyo...  14.7 us
    unnamed x18, local copies, waits for them, and re-layouts  8.11 us
    all_to_all x1, waiting for transfers between devices, body(): lax.all_to_all(local_squares(out_grad, val_grad, everyone).reshape(everyo...  7.57 us
    pallas_call x1, Pallas kernels, next_momentum(): pl.pallas_call(next_kernel, grid=(steps,), in_specs=[pl.BlockSpec((8, LAN...  7.06 us
    all_to_all x1, starting transfers between devices, body(): lax.all_to_all(back.reshape(heads, given // 2, 2, LANES), 'dp', split_axi...  5.56 us
    pallas_call x1, Pallas kernels, orthogonalize(): pl.pallas_call(functools.partial(orthogonal_kernel, sizes), in_specs=[VME...  4.06 us
  transfers between devices with their start and end apart: 2, of which 2 were waited for; matrix products, arithmetic and copies ran while one was open for 0% of the time, Pallas kernels for 5%

profile of v1, /device:TPU:2, one launch (start us, length us, event | category | flops | bytes accessed | tf_op | source)
XLA Modules:
  0.0 156.1 jit_solution(17697446336826197746)
XLA Ops:
  0.6 0.0 copy-start.6
  0.6 2.9 %squares.1 = f32[256,128]{1,0:T(8,128)} custom-call(bf16[64,112,128]{2,1,0:T(8,128)(2,1)} %bitcast.54, bf16[64,16,128]{2,1,0:T(8,128)(2,1)} %bitcast.61), custom_call_target="tpu_custom_call" | custom-call | tf_op jit(solution)/shard_map/squares/pallas_call | solution.py:69
  3.6 14.7 %all-to-all-start = ((f32[256,1,128]{2,1,0:T(1,128)}), f32[256,1,128]{2,1,0:T(1,128)S(1)}, u32[]{:S(2)}, u32[]{:S(2)}) async-start(f32[256,1,128]{2,1,0:T(1,128)} %bitcast.67), calls=%async_computation | async-start | bytes 262144 | tf_op jit(solution)/shard_map/all_to_all | solution.py:313
  18.3 0.0 copy-done.6
  18.3 0.0 copy-start.3
  18.3 2.0 %copy-done.3 = f32[1,64,2,7168]{3,2,1,0:T(2,128)S(1)} copy-done((f32[1,64,2,7168]{3,2,1,0:T(2,128)S(1)}, f32[1,64,2,7168]{3,2,1,0:T(2,128)}, u32[]{:S(2)}) %copy-start.3) | copy-done | bytes 3670040
  20.3 0.0 copy-start.2
  20.3 0.0 copy-start.5
  20.3 0.4 prepare.1.decayed_ref
  20.7 0.0 copy-start
  20.7 1.9 %copy-done = f32[64,128,128]{2,1,0:T(8,128)} copy-done((f32[64,128,128]{2,1,0:T(8,128)}, f32[64,128,128]{2,1,0:T(8,128)S(1)}, u32[]{:S(2)}) %copy-start) | copy-done | bytes 4194328
  22.7 7.6 %all-to-all-done = f32[256,1,128]{2,1,0:T(1,128)S(1)} async-done(((f32[256,1,128]{2,1,0:T(1,128)}), f32[256,1,128]{2,1,0:T(1,128)S(1)}, u32[]{:S(2)}, u32[]{:S(2)}) %all-to-all-start) | async-done | bytes 131104 | tf_op jit(solution)/shard_map/all_to_all | solution.py:313
  30.2 0.0 copy-done.2
  30.2 0.0 copy-done.5
  30.2 0.0 copy-start.1
  30.2 2.2 %copy-done.1 = f32[64,128,128]{2,1,0:T(8,128)S(1)} copy-done((f32[64,128,128]{2,1,0:T(8,128)S(1)}, f32[64,128,128]{2,1,0:T(8,128)}, u32[]{:S(2)}) %copy-start.1) | copy-done | bytes 4194328
  32.4 1.3 send.1
  33.7 0.0 copy-start.7
  33.7 0.6 copy-done.7
  34.3 56.4 %all_to_all.15.got_ref = bf16[64,128,128]{2,1,0:T(8,128)(2,1)S(1)} all-to-all(bf16[64,128,128]{2,1,0:T(8,128)(2,1)S(1)} %get-tuple-element.12), channel_id=1, replica_groups=mesh['dp'=64,'layer'=4] {'dp'}, dimensions={0} | all-to-all | bytes 4194304 | tf_op jit(solution)/shard_map/all_to_all | solution.py:325
  90.7 4.1 %orthogonal.1 = bf16[8320,128]{1,0:T(8,128)(2,1)S(1)} custom-call(bf16[64,128,128]{2,1,0:T(8,128)(2,1)S(1)} %all_to_all.15.got_ref), custom_call_target="tpu_custom_call" | custom-call | tf_op jit(solution)/shard_map/orthogonal/pallas_call | solution.py:237
  94.8 0.0 copy-start.4
  94.8 1.3 copy-done.4
  96.1 0.0 copy-start.8
  96.1 5.6 %all-to-all-start.2 = ((bf16[64,65,2,128]{3,2,1,0:T(2,128)(2,1)}), bf16[64,65,2,128]{3,2,1,0:T(2,128)(2,1)S(1)}, u32[]{:S(2)}, u32[]{:S(2)}) async-start(bf16[64,65,2,128]{3,2,1,0:T(2,128)(2,1)} %bitcast.60), calls=%async_computation.2 | async-start | bytes 4259840 | tf_op jit(solution)/shard_map/all_to_all | solution.py:330
  101.7 0.0 copy-done.8
  101.7 0.1 copy.36
  101.9 0.1 multiply_reduce_fusion
  102.0 0.1 copy.37
  102.1 0.2 and_convert_fusion.choice_ref
  102.3 7.1 %next.1 = (f32[64,112,128]{2,1,0:T(8,128)}, f32[64,16,128]{2,1,0:T(8,128)}) custom-call(f32[8,128]{1,0:T(8,128)} %copy-done.7, bf16[64,112,128]{2,1,0:T(8,128)(2,1)} %bitcast.55, f32[64,112,128]{2,1,0:T(8,128)} %bitcast.57, bf16[64,16,128]{2,1,0:T(8,128)(2,1)} %bitcast.62, f32[64,16,128]{2,1,0:T(8,128)} %bitcast.64), custom_call_target="tpu_custom_call" | custom-call | tf_op jit(solution)/shard_map/next/pallas_call | solution.py:141
  109.3 44.3 %all-to-all-done.2 = bf16[64,65,2,128]{3,2,1,0:T(2,128)(2,1)S(1)} async-done(((bf16[64,65,2,128]{3,2,1,0:T(2,128)(2,1)}), bf16[64,65,2,128]{3,2,1,0:T(2,128)(2,1)S(1)}, u32[]{:S(2)}, u32[]{:S(2)}) %all-to-all-start.2) | async-done | bytes 2129952 | tf_op jit(solution)/shard_map/all_to_all | solution.py:330
  153.7 2.4 %finish.1 = (bf16[64,112,128]{2,1,0:T(8,128)(2,1)}, bf16[64,16,128]{2,1,0:T(8,128)(2,1)}, f32[2,128]{1,0:T(2,128)}) custom-call(bf16[8320,128]{1,0:T(8,128)(2,1)S(1)} %bitcast.59, f32[64,2,128]{2,1,0:T(2,128)S(1)} %and_convert_fusion.choice_ref), custom_call_target="tpu_custom_call" | custom-call | tf_op jit(solution)/shard_map/finish/pallas_call | solution.py:279
  (3 shorter events, 0.0 us)
Async XLA Ops:
  0.6 17.7 %copy-start.6 = (f32[1,64,4,512]{3,2,1,0:T(4,128)S(1)}, f32[1,64,4,512]{3,2,1,0:T(4,128)}, u32[]{:S(2)}) copy-start(f32[1,64,4,512]{3,2,1,0:T(4,128)} %param.8) | copy-start | bytes 1572868
  3.6 26.6 %all-to-all-start = ((f32[256,1,128]{2,1,0:T(1,128)}), f32[256,1,128]{2,1,0:T(1,128)S(1)}, u32[]{:S(2)}, u32[]{:S(2)}) async-start(f32[256,1,128]{2,1,0:T(1,128)} %bitcast.67), calls=%async_computation | async-start | bytes 262144 | tf_op jit(solution)/shard_map/all_to_all | solution.py:313
  18.3 2.0 %copy-start.3 = (f32[1,64,2,7168]{3,2,1,0:T(2,128)S(1)}, f32[1,64,2,7168]{3,2,1,0:T(2,128)}, u32[]{:S(2)}) copy-start(f32[1,64,2,7168]{3,2,1,0:T(2,128)} %param.6) | copy-start | bytes 11010052
  20.3 9.9 %copy-start.2 = (bf16[1,64,2,7168]{3,2,1,0:T(2,128)(2,1)S(1)}, bf16[1,64,2,7168]{3,2,1,0:T(2,128)(2,1)}, u32[]{:S(2)}) copy-start(bf16[1,64,2,7168]{3,2,1,0:T(2,128)(2,1)} %param.5) | copy-start | bytes 5505028
  20.3 9.9 %copy-start.5 = (bf16[1,64,4,512]{3,2,1,0:T(4,128)(2,1)S(1)}, bf16[1,64,4,512]{3,2,1,0:T(4,128)(2,1)}, u32[]{:S(2)}) copy-start(bf16[1,64,4,512]{3,2,1,0:T(4,128)(2,1)} %param.7) | copy-start | bytes 786436
  20.7 1.9 %copy-start = (f32[64,128,128]{2,1,0:T(8,128)}, f32[64,128,128]{2,1,0:T(8,128)S(1)}, u32[]{:S(2)}) copy-start(f32[64,128,128]{2,1,0:T(8,128)S(1)} %prepare.1.decayed_ref) | copy-start | bytes 12582916
  30.2 2.2 %copy-start.1 = (f32[64,128,128]{2,1,0:T(8,128)S(1)}, f32[64,128,128]{2,1,0:T(8,128)}, u32[]{:S(2)}) copy-start(f32[64,128,128]{2,1,0:T(8,128)} %copy-done) | copy-start | bytes 12582916
  33.7 0.6 copy-start.7
  94.8 1.3 copy-start.4
  96.1 5.6 %copy-start.8 = (s32[1,2,64,1]{2,3,1,0:T(1,128)S(1)}, s32[1,2,64,1]{2,3,1,0:T(1,128)}, u32[]{:S(2)}) copy-start(s32[1,2,64,1]{2,3,1,0:T(1,128)} %param.9) | copy-start | bytes 1540
  96.1 57.5 %all-to-all-start.2 = ((bf16[64,65,2,128]{3,2,1,0:T(2,128)(2,1)}), bf16[64,65,2,128]{3,2,1,0:T(2,128)(2,1)S(1)}, u32[]{:S(2)}, u32[]{:S(2)}) async-start(bf16[64,65,2,128]{3,2,1,0:T(2,128)(2,1)} %bitcast.60), calls=%async_computation.2 | async-start | bytes 4259840 | tf_op jit(solution)/shard_map/all_to_all | solution.py:330

commit v2 on v1

--- a/solution.py
+++ b/solution.py
@@ -76,9 +76,9 @@
             pltpu.VMEM(val_grad.shape, BF16),
             pltpu.SemaphoreType.DMA((2, CHUNKS)),
         ],
-        compiler_params=pltpu.CompilerParams(vmem_limit_bytes=GRANT),
+        compiler_params=pltpu.CompilerParams(vmem_limit_bytes=16 * 1024 * 1024),
         name="squares",
-    )(out_grad, val_grad)
+    )(*(pltpu.with_memory_space_constraint(x, pltpu.HBM) for x in (out_grad, val_grad)))
 
 
 def prepare_kernel(om_ref, vm_ref, decayed_ref):
@@ -100,29 +100,51 @@
     )(out_momentum, val_momentum)
 
 
+def row_sum_kernel(parts_ref, sum_ref):
+    sum_ref[...] = jnp.broadcast_to(jnp.sum(parts_ref[...], axis=0, keepdims=True), sum_ref.shape)
+
+
+def row_sum(parts):
+    return pl.pallas_call(
+        row_sum_kernel,
+        in_specs=[VMEM],
+        out_specs=VMEM,
+        out_shape=jax.ShapeDtypeStruct((8, LANES), F32),
+        compiler_params=pltpu.CompilerParams(vmem_limit_bytes=4 * 1024 * 1024),
+        name="row_sum",
+    )(parts)
+
+
 def clip_of(parts, count):
     total = jnp.sum(jnp.sum(parts, axis=0, keepdims=True), axis=1, keepdims=True)
     return jnp.minimum(1.0, CLIP_RMS * math.sqrt(count) / jnp.sqrt(total + 1e-06))
 
 
-def send_kernel(count, parts_ref, og_ref, vg_ref, decayed_ref, send_ref, clip_ref):
-    clip = jnp.broadcast_to(clip_of(parts_ref[...], count), clip_ref.shape)
+def send_kernel(count, layers, *refs):
+    parts_refs, refs = refs[:layers], refs[layers:]
+    og_ref, vg_ref, decayed_ref, send_ref, clip_hbm, clip_ref, clip_sem = refs
+    parts = jnp.concatenate([ref[0:1, :] for ref in parts_refs], axis=0)
+    clip = jnp.broadcast_to(clip_of(parts, count), clip_ref.shape)
     clip_ref[...] = clip
+    copy = pltpu.make_async_copy(clip_ref, clip_hbm, clip_sem)
+    copy.start()
     factor = ((1.0 + MOMENT) * clip[0:1]).reshape(1, 1, LANES)
     depth = og_ref.shape[1]
     send_ref[:, :depth, :] = (factor * og_ref[...].astype(F32) + decayed_ref[:, :depth, :]).astype(BF16)
     send_ref[:, depth:, :] = (factor * vg_ref[...].astype(F32) + decayed_ref[:, depth:, :]).astype(BF16)
+    copy.wait()
 
 
 def rows_to_send(parts, count, out_grad, val_grad, decayed):
     return pl.pallas_call(
-        functools.partial(send_kernel, count),
-        in_specs=[VMEM] * 4,
-        out_specs=[VMEM, VMEM],
-        out_shape=[jax.ShapeDtypeStruct(decayed.shape, BF16), jax.ShapeDtypeStruct((8, LANES), F32)],
+        functools.partial(send_kernel, count, len(parts)),
+        in_specs=[VMEM] * (len(parts) + 3),
+        out_specs=[VMEM, HBM],
+        out_shape=[jax.ShapeDtypeStruct(decayed.shape, BF16), pltpu.HBM((8, LANES), F32)],
+        scratch_shapes=[pltpu.VMEM((8, LANES), F32), pltpu.SemaphoreType.DMA(())],
         compiler_params=pltpu.CompilerParams(vmem_limit_bytes=24 * 1024 * 1024),
         name="send",
-    )(parts, out_grad, val_grad, decayed)
+    )(*parts, out_grad, val_grad, decayed)
 
 
 def next_kernel(clip_ref, og_ref, om_ref, vg_ref, vm_ref, on_ref, vn_ref):
@@ -238,7 +260,7 @@
         functools.partial(orthogonal_kernel, sizes),
         in_specs=[VMEM],
         out_specs=HBM,
-        out_shape=jax.ShapeDtypeStruct((sources * given, LANES), BF16),
+        out_shape=pltpu.HBM((sources * given, LANES), BF16),
         scratch_shapes=[pltpu.VMEM((sources * pitch, LANES), F32), pltpu.VMEM((sources * given, LANES), BF16)]
         + [pltpu.VMEM((rows * sources, columns), BF16) for rows, columns in sizes]
         + [pltpu.SemaphoreType.DMA((CHUNKS,))],
@@ -311,15 +333,20 @@
 
     everyone = owners * layers
     parts = lax.all_to_all(
-        local_squares(out_grad, val_grad, everyone).reshape(everyone, 1, LANES),
-        ("dp", "layer"),
+        local_squares(out_grad, val_grad, owners).reshape(owners, 1, LANES),
+        "dp",
         split_axis=0,
         concat_axis=0,
         tiled=True,
-    ).reshape(everyone, LANES)
+    ).reshape(owners, LANES)
+    mine = row_sum(parts)
+    mine, *momenta = lax.optimization_barrier((mine, out_momentum, val_momentum))
+    decayed = prepare(*momenta)
+    parts = [mine] + [
+        lax.ppermute(mine, "layer", [(i, (i + shift) % layers) for i in range(layers)]) for shift in range(1, layers)
+    ]
     count = (output_grad.size + values_grad.size) * everyone
 
-    decayed = prepare(out_momentum, val_momentum)
     send, clip = rows_to_send(parts, count, out_grad, val_grad, decayed)
     out_next, val_next = next_momentum(clip, out_grad, out_momentum, val_grad, val_momentum)
     got = lax.all_to_all(send, "dp", split_axis=0, concat_axis=0, tiled=True)

time: 157 us -> 155 us (0.987)
  blocking collectives: 56.4 us -> 76.5 us
  starting transfers between devices: 20.3 us -> 11.3 us
  waiting for transfers between devices: 51.9 us -> 44.3 us
  local copies, waits for them, and re-layouts: 8.32 us -> 2.81 us
    all_to_all x0 -> x1, blocking collectives: none -> 20.4 us  [body(): lax.all_to_all(local_squares(out_grad, val_grad, owners).reshape(owners,...]
    all_to_all x1 -> x0, starting transfers between devices: 14.7 us -> none  [body(): lax.all_to_all(local_squares(out_grad, val_grad, everyone).reshape(everyo...]
    all_to_all x1 -> x0, waiting for transfers between devices: 7.57 us -> none  [body(): lax.all_to_all(local_squares(out_grad, val_grad, everyone).reshape(everyo...]
    ppermute x0 -> x3, starting transfers between devices: none -> 5.9 us  [body(): lax.ppermute(mine, 'layer', [(i, (i + shift) % layers) for i in range(lay...]
    unnamed x18 -> x10, local copies, waits for them, and re-layouts: 8.11 us -> 2.6 us
  transfers between devices with their start and end apart: 2 -> 4, of which waited for: 2 -> 1; matrix products, arithmetic and copies ran while one was open for 0% -> 0% of each run, Pallas kernels for 5% -> 5%
where the time goes in v2:
time: 155 us
  blocking collectives  76.5 us (49%)
  waiting for transfers between devices  44.3 us (29%)
  Pallas kernels  18.5 us (12%)
  starting transfers between devices  11.3 us (7%)
  local copies, waits for them, and re-layouts  2.81 us (2%)
    all_to_all x1, blocking collectives, body(): got = lax.all_to_all(send, 'dp', split_axis=0, concat_axis=0, tiled=True)  56.1 us
    all_to_all x1, waiting for transfers between devices, body(): lax.all_to_all(back.reshape(heads, given // 2, 2, LANES), 'dp', split_axi...  44.3 us
    all_to_all x1, blocking collectives, body(): lax.all_to_all(local_squares(out_grad, val_grad, owners).reshape(owners,...  20.4 us
    pallas_call x1, Pallas kernels, next_momentum(): pl.pallas_call(next_kernel, grid=(steps,), in_specs=[pl.BlockSpec((8, LAN...  7.06 us
    ppermute x3, starting transfers between devices, body(): lax.ppermute(mine, 'layer', [(i, (i + shift) % layers) for i in range(lay...  5.9 us
    all_to_all x1, starting transfers between devices, body(): lax.all_to_all(back.reshape(heads, given // 2, 2, LANES), 'dp', split_axi...  5.44 us
    pallas_call x1, Pallas kernels, orthogonalize(): pl.pallas_call(functools.partial(orthogonal_kernel, sizes), in_specs=[VME...  5.07 us
  transfers between devices with their start and end apart: 4, of which 1 were waited for; matrix products, arithmetic and copies ran while one was open for 0% of the time, Pallas kernels for 5%

profile of v2, /device:TPU:2, one launch (start us, length us, event | category | flops | bytes accessed | tf_op | source)
XLA Modules:
  0.0 154.6 jit_solution(393171727245051541)
XLA Ops:
  0.6 0.0 copy-start.3
  0.6 2.3 %squares.1 = f32[64,128]{1,0:T(8,128)S(1)} custom-call(bf16[64,112,128]{2,1,0:T(8,128)(2,1)} %bitcast.54, bf16[64,16,128]{2,1,0:T(8,128)(2,1)} %bitcast.60), custom_call_target="tpu_custom_call" | custom-call | tf_op jit(solution)/shard_map/squares/pallas_call | solution.py:69
  2.9 20.4 %all_to_all.15 = f32[64,1,128]{2,1,0:T(1,128)S(1)} all-to-all(f32[64,1,128]{2,1,0:T(1,128)S(1)} %bitcast.65), channel_id=1, replica_groups=mesh['dp'=64,'layer'=4] {'dp'}, dimensions={0} | all-to-all | bytes 65536 | tf_op jit(solution)/shard_map/all_to_all | solution.py:335
  23.4 0.0 copy-start
  23.4 1.7 %collective-permute-start = (f32[8,128]{1,0:T(8,128)S(1)}, f32[8,128]{1,0:T(8,128)S(1)}, u32[]{:S(2)}, u32[]{:S(2)}) collective-permute-start(f32[8,128]{1,0:T(8,128)S(1)} %row_sum.1.refs_0_), channel_id=1, source_target_pairs={{0,1},{1,2},{2,3},{3,0},{4,5},{5,6},{6,7},{7,4},{8,9},{9,10},{10,1... | collective-permute-start | bytes 12296 | tf_op jit(solution)/shard_map/ppermute | solution.py:346
  25.0 2.9 %collective-permute-start.1 = (f32[8,128]{1,0:T(8,128)S(1)}, f32[8,128]{1,0:T(8,128)S(1)}, u32[]{:S(2)}, u32[]{:S(2)}) collective-permute-start(f32[8,128]{1,0:T(8,128)S(1)} %row_sum.1.refs_0_), channel_id=1, source_target_pairs={{0,2},{1,3},{2,0},{3,1},{4,6},{5,7},{6,4},{7,5},{8,10},{9,11},{10,... | collective-permute-start | bytes 12296 | tf_op jit(solution)/shard_map/ppermute | solution.py:346
  27.9 1.3 collective-permute-start.2
  29.3 0.0 copy-done.3
  29.3 0.0 copy-start.1
  29.3 2.0 %copy-done.1 = f32[1,64,2,7168]{3,2,1,0:T(2,128)S(1)} copy-done((f32[1,64,2,7168]{3,2,1,0:T(2,128)S(1)}, f32[1,64,2,7168]{3,2,1,0:T(2,128)}, u32[]{:S(2)}) %copy-start.1) | copy-done | bytes 3670040
  31.3 0.0 copy-start.2
  31.3 0.4 prepare.1.refs_6_
  31.7 0.0 collective-permute-done.refs_1_
  31.7 0.0 collective-permute-done.1.refs_2_
  31.7 0.0 collective-permute-done.2.refs_3_
  31.7 0.0 copy-done
  31.7 0.5 copy-done.2
  32.3 1.3 send.1
  33.5 56.1 %all_to_all.16.got_ref = bf16[64,128,128]{2,1,0:T(8,128)(2,1)S(1)} all-to-all(bf16[64,128,128]{2,1,0:T(8,128)(2,1)S(1)} %get-tuple-element.18), channel_id=1, replica_groups=mesh['dp'=64,'layer'=4] {'dp'}, dimensions={0} | all-to-all | bytes 4194304 | tf_op jit(solution)/shard_map/all_to_all | solution.py:352
  89.6 5.1 %orthogonal.1 = bf16[8320,128]{1,0:T(8,128)(2,1)} custom-call(bf16[64,128,128]{2,1,0:T(8,128)(2,1)S(1)} %all_to_all.16.got_ref), custom_call_target="tpu_custom_call" | custom-call | tf_op jit(solution)/shard_map/orthogonal/pallas_call | solution.py:259
  94.7 0.0 copy-start.4
  94.7 5.4 %all-to-all-start.2 = ((bf16[64,65,2,128]{3,2,1,0:T(2,128)(2,1)}), bf16[64,65,2,128]{3,2,1,0:T(2,128)(2,1)S(1)}, u32[]{:S(2)}, u32[]{:S(2)}) async-start(bf16[64,65,2,128]{3,2,1,0:T(2,128)(2,1)} %bitcast.67), calls=%async_computation.2 | async-start | bytes 4259840 | tf_op jit(solution)/shard_map/all_to_all | solution.py:357
  100.2 0.0 copy-done.4
  100.2 0.1 multiply_reduce_fusion
  100.3 0.1 copy.37
  100.5 0.1 copy.36
  100.6 0.2 and_convert_fusion.choice_ref
  100.8 7.1 %next.1 = (f32[64,112,128]{2,1,0:T(8,128)}, f32[64,16,128]{2,1,0:T(8,128)}) custom-call(f32[8,128]{1,0:T(8,128)} %get-tuple-element.20.clip_ref, bf16[64,112,128]{2,1,0:T(8,128)(2,1)} %bitcast.55, f32[64,112,128]{2,1,0:T(8,128)} %bitcast.57, bf16[64,16,128]{2,1,0:T(8,128)(2,1)} %bitcast.61, f32[64,16,128]{2,1,0:T(8,128)} %bitcast.63), custom_call_target="tpu_custom_call" | custom-call | tf_op jit(solution)/shard_map/next/pallas_call | solution.py:163
  107.8 44.3 %all-to-all-done.2 = bf16[64,65,2,128]{3,2,1,0:T(2,128)(2,1)S(1)} async-done(((bf16[64,65,2,128]{3,2,1,0:T(2,128)(2,1)}), bf16[64,65,2,128]{3,2,1,0:T(2,128)(2,1)S(1)}, u32[]{:S(2)}, u32[]{:S(2)}) %all-to-all-start.2) | async-done | bytes 2129952 | tf_op jit(solution)/shard_map/all_to_all | solution.py:357
  152.2 2.4 %finish.1 = (bf16[64,112,128]{2,1,0:T(8,128)(2,1)}, bf16[64,16,128]{2,1,0:T(8,128)(2,1)}, f32[2,128]{1,0:T(2,128)}) custom-call(bf16[8320,128]{1,0:T(8,128)(2,1)S(1)} %bitcast.59, f32[64,2,128]{2,1,0:T(2,128)S(1)} %and_convert_fusion.choice_ref), custom_call_target="tpu_custom_call" | custom-call | tf_op jit(solution)/shard_map/finish/pallas_call | solution.py:301
  (4 shorter events, 0.0 us)
Async XLA Ops:
  0.6 28.6 %copy-start.3 = (f32[1,64,4,512]{3,2,1,0:T(4,128)S(1)}, f32[1,64,4,512]{3,2,1,0:T(4,128)}, u32[]{:S(2)}) copy-start(f32[1,64,4,512]{3,2,1,0:T(4,128)} %param.8) | copy-start | bytes 1572868
  23.4 8.4 %copy-start = (bf16[1,64,2,7168]{3,2,1,0:T(2,128)(2,1)S(1)}, bf16[1,64,2,7168]{3,2,1,0:T(2,128)(2,1)}, u32[]{:S(2)}) copy-start(bf16[1,64,2,7168]{3,2,1,0:T(2,128)(2,1)} %param.5) | copy-start | bytes 5505028
  23.4 8.3 %collective-permute-start = (f32[8,128]{1,0:T(8,128)S(1)}, f32[8,128]{1,0:T(8,128)S(1)}, u32[]{:S(2)}, u32[]{:S(2)}) collective-permute-start(f32[8,128]{1,0:T(8,128)S(1)} %row_sum.1.refs_0_), channel_id=1, source_target_pairs={{0,1},{1,2},{2,3},{3,0},{4,5},{5,6},{6,7},{7,4},{8,9},{9,10},{10,1... | collective-permute-start | bytes 12296 | tf_op jit(solution)/shard_map/ppermute | solution.py:346
  25.0 6.7 %collective-permute-start.1 = (f32[8,128]{1,0:T(8,128)S(1)}, f32[8,128]{1,0:T(8,128)S(1)}, u32[]{:S(2)}, u32[]{:S(2)}) collective-permute-start(f32[8,128]{1,0:T(8,128)S(1)} %row_sum.1.refs_0_), channel_id=1, source_target_pairs={{0,2},{1,3},{2,0},{3,1},{4,6},{5,7},{6,4},{7,5},{8,10},{9,11},{10,... | collective-permute-start | bytes 12296 | tf_op jit(solution)/shard_map/ppermute | solution.py:346
  27.9 3.8 %collective-permute-start.2 = (f32[8,128]{1,0:T(8,128)S(1)}, f32[8,128]{1,0:T(8,128)S(1)}, u32[]{:S(2)}, u32[]{:S(2)}) collective-permute-start(f32[8,128]{1,0:T(8,128)S(1)} %row_sum.1.refs_0_), channel_id=1, source_target_pairs={{0,3},{1,0},{2,1},{3,2},{4,7},{5,4},{6,5},{7,6},{8,11},{9,8},{10,9... | collective-permute-start | bytes 12296 | tf_op jit(solution)/shard_map/ppermute | solution.py:346
  29.3 2.0 %copy-start.1 = (f32[1,64,2,7168]{3,2,1,0:T(2,128)S(1)}, f32[1,64,2,7168]{3,2,1,0:T(2,128)}, u32[]{:S(2)}) copy-start(f32[1,64,2,7168]{3,2,1,0:T(2,128)} %param.6) | copy-start | bytes 11010052
  31.3 0.9 copy-start.2
  94.7 5.5 %copy-start.4 = (s32[1,2,64,1]{2,3,1,0:T(1,128)S(1)}, s32[1,2,64,1]{2,3,1,0:T(1,128)}, u32[]{:S(2)}) copy-start(s32[1,2,64,1]{2,3,1,0:T(1,128)} %param.9) | copy-start | bytes 1540
  94.7 57.4 %all-to-all-start.2 = ((bf16[64,65,2,128]{3,2,1,0:T(2,128)(2,1)}), bf16[64,65,2,128]{3,2,1,0:T(2,128)(2,1)S(1)}, u32[]{:S(2)}, u32[]{:S(2)}) async-start(bf16[64,65,2,128]{3,2,1,0:T(2,128)(2,1)} %bitcast.67), calls=%async_computation.2 | async-start | bytes 4259840 | tf_op jit(solution)/shard_map/all_to_all | solution.py:357

commit v3 on v2

--- a/solution.py
+++ b/solution.py
@@ -69,13 +69,9 @@
     return pl.pallas_call(
         squares_kernel,
         in_specs=[HBM, HBM],
-        out_specs=VMEM,
-        out_shape=jax.ShapeDtypeStruct((pieces, LANES), F32),
-        scratch_shapes=[
-            pltpu.VMEM(out_grad.shape, BF16),
-            pltpu.VMEM(val_grad.shape, BF16),
-            pltpu.SemaphoreType.DMA((2, CHUNKS)),
-        ],
+        out_specs=[VMEM] * 3,
+        out_shape=[pltpu.VMEM((pieces, LANES), F32)] + [pltpu.VMEM(x.shape, BF16) for x in (out_grad, val_grad)],
+        scratch_shapes=[pltpu.SemaphoreType.DMA((2, CHUNKS))],
         compiler_params=pltpu.CompilerParams(vmem_limit_bytes=16 * 1024 * 1024),
         name="squares",
     )(*(pltpu.with_memory_space_constraint(x, pltpu.HBM) for x in (out_grad, val_grad)))
@@ -332,8 +328,9 @@
     heads = out_grad.shape[0]
 
     everyone = owners * layers
+    squares, out_near, val_near = local_squares(out_grad, val_grad, owners)
     parts = lax.all_to_all(
-        local_squares(out_grad, val_grad, owners).reshape(owners, 1, LANES),
+        squares.reshape(owners, 1, LANES),
         "dp",
         split_axis=0,
         concat_axis=0,
@@ -347,7 +344,7 @@
     ]
     count = (output_grad.size + values_grad.size) * everyone
 
-    send, clip = rows_to_send(parts, count, out_grad, val_grad, decayed)
+    send, clip = rows_to_send(parts, count, out_near, val_near, decayed)
     out_next, val_next = next_momentum(clip, out_grad, out_momentum, val_grad, val_momentum)
     got = lax.all_to_all(send, "dp", split_axis=0, concat_axis=0, tiled=True)
 

time: 155 us -> 154 us (level)
  no operation moved by 1% of the time
where the time goes in v3:
time: 154 us
  blocking collectives  76.5 us (50%)
  waiting for transfers between devices  44.3 us (29%)
  Pallas kernels  18.5 us (12%)
  starting transfers between devices  11.3 us (7%)
  local copies, waits for them, and re-layouts  2.26 us (1%)
    all_to_all x1, blocking collectives, body(): got = lax.all_to_all(send, 'dp', split_axis=0, concat_axis=0, tiled=True)  56.1 us
    all_to_all x1, waiting for transfers between devices, body(): lax.all_to_all(back.reshape(heads, given // 2, 2, LANES), 'dp', split_axi...  44.3 us
    all_to_all x1, blocking collectives, body(): lax.all_to_all(squares.reshape(owners, 1, LANES), 'dp', split_axis=0, con...  20.4 us
    pallas_call x1, Pallas kernels, next_momentum(): pl.pallas_call(next_kernel, grid=(steps,), in_specs=[pl.BlockSpec((8, LAN...  7.06 us
    ppermute x3, starting transfers between devices, body(): lax.ppermute(mine, 'layer', [(i, (i + shift) % layers) for i in range(lay...  5.9 us
    all_to_all x1, starting transfers between devices, body(): lax.all_to_all(back.reshape(heads, given // 2, 2, LANES), 'dp', split_axi...  5.44 us
    pallas_call x1, Pallas kernels, orthogonalize(): pl.pallas_call(functools.partial(orthogonal_kernel, sizes), in_specs=[VME...  5.07 us
  transfers between devices with their start and end apart: 4, of which 1 were waited for; matrix products, arithmetic and copies ran while one was open for 0% of the time, Pallas kernels for 5%

profile of v3, /device:TPU:2, one launch (start us, length us, event | category | flops | bytes accessed | tf_op | source)
XLA Modules:
  0.0 154.0 jit_solution(14899150464625859085)
XLA Ops:
  0.6 0.0 copy-start.1
  0.6 2.3 %squares.1 = (f32[64,128]{1,0:T(8,128)S(1)}, bf16[64,112,128]{2,1,0:T(8,128)(2,1)S(1)}, bf16[64,16,128]{2,1,0:T(8,128)(2,1)S(1)}) custom-call(bf16[64,112,128]{2,1,0:T(8,128)(2,1)} %bitcast.62, bf16[64,16,128]{2,1,0:T(8,128)(2,1)} %bitcast.64), custom_call_target="tpu_custom_call" | custom-call | tf_op jit(solution)/shard_map/squares/pallas_call | solution.py:69
  2.9 20.4 %all_to_all.15 = f32[64,1,128]{2,1,0:T(1,128)S(1)} all-to-all(f32[64,1,128]{2,1,0:T(1,128)S(1)} %bitcast.60), channel_id=1, replica_groups=mesh['dp'=64,'layer'=4] {'dp'}, dimensions={0} | all-to-all | bytes 65536 | tf_op jit(solution)/shard_map/all_to_all | solution.py:332
  23.4 1.7 %collective-permute-start = (f32[8,128]{1,0:T(8,128)S(1)}, f32[8,128]{1,0:T(8,128)S(1)}, u32[]{:S(2)}, u32[]{:S(2)}) collective-permute-start(f32[8,128]{1,0:T(8,128)S(1)} %row_sum.1.refs_0_), channel_id=1, source_target_pairs={{0,1},{1,2},{2,3},{3,0},{4,5},{5,6},{6,7},{7,4},{8,9},{9,10},{10,1... | collective-permute-start | bytes 12296 | tf_op jit(solution)/shard_map/ppermute | solution.py:343
  25.0 2.9 %collective-permute-start.1 = (f32[8,128]{1,0:T(8,128)S(1)}, f32[8,128]{1,0:T(8,128)S(1)}, u32[]{:S(2)}, u32[]{:S(2)}) collective-permute-start(f32[8,128]{1,0:T(8,128)S(1)} %row_sum.1.refs_0_), channel_id=1, source_target_pairs={{0,2},{1,3},{2,0},{3,1},{4,6},{5,7},{6,4},{7,5},{8,10},{9,11},{10,... | collective-permute-start | bytes 12296 | tf_op jit(solution)/shard_map/ppermute | solution.py:343
  27.9 1.3 collective-permute-start.2
  29.3 0.0 copy-done.1
  29.3 0.0 copy-start
  29.3 2.0 %copy-done = f32[1,64,2,7168]{3,2,1,0:T(2,128)S(1)} copy-done((f32[1,64,2,7168]{3,2,1,0:T(2,128)S(1)}, f32[1,64,2,7168]{3,2,1,0:T(2,128)}, u32[]{:S(2)}) %copy-start) | copy-done | bytes 3670040
  31.3 0.4 prepare.1.refs_6_
  31.7 0.0 collective-permute-done.refs_1_
  31.7 0.0 collective-permute-done.1.refs_2_
  31.7 0.0 collective-permute-done.2.refs_3_
  31.7 1.3 send.1
  33.0 56.1 %all_to_all.16.got_ref = bf16[64,128,128]{2,1,0:T(8,128)(2,1)S(1)} all-to-all(bf16[64,128,128]{2,1,0:T(8,128)(2,1)S(1)} %get-tuple-element.24), channel_id=1, replica_groups=mesh['dp'=64,'layer'=4] {'dp'}, dimensions={0} | all-to-all | bytes 4194304 | tf_op jit(solution)/shard_map/all_to_all | solution.py:349
  89.1 5.1 %orthogonal.1 = bf16[8320,128]{1,0:T(8,128)(2,1)} custom-call(bf16[64,128,128]{2,1,0:T(8,128)(2,1)S(1)} %all_to_all.16.got_ref), custom_call_target="tpu_custom_call" | custom-call | tf_op jit(solution)/shard_map/orthogonal/pallas_call | solution.py:255
  94.2 0.0 copy-start.2
  94.2 5.4 %all-to-all-start.2 = ((bf16[64,65,2,128]{3,2,1,0:T(2,128)(2,1)}), bf16[64,65,2,128]{3,2,1,0:T(2,128)(2,1)S(1)}, u32[]{:S(2)}, u32[]{:S(2)}) async-start(bf16[64,65,2,128]{3,2,1,0:T(2,128)(2,1)} %bitcast.61), calls=%async_computation.2 | async-start | bytes 4259840 | tf_op jit(solution)/shard_map/all_to_all | solution.py:354
  99.6 0.0 copy-done.2
  99.7 0.1 multiply_reduce_fusion
  99.8 0.1 copy.37
  99.9 0.1 copy.36
  100.0 0.2 and_convert_fusion.choice_ref
  100.2 7.1 %next.1 = (f32[64,112,128]{2,1,0:T(8,128)}, f32[64,16,128]{2,1,0:T(8,128)}) custom-call(f32[8,128]{1,0:T(8,128)} %get-tuple-element.26.clip_ref, bf16[64,112,128]{2,1,0:T(8,128)(2,1)} %bitcast.63, f32[64,112,128]{2,1,0:T(8,128)} %bitcast.54, bf16[64,16,128]{2,1,0:T(8,128)(2,1)} %bitcast.65, f32[64,16,128]{2,1,0:T(8,128)} %bitcast.57), custom_call_target="tpu_custom_call" | custom-call | tf_op jit(solution)/shard_map/next/pallas_call | solution.py:159
  107.3 44.3 %all-to-all-done.2 = bf16[64,65,2,128]{3,2,1,0:T(2,128)(2,1)S(1)} async-done(((bf16[64,65,2,128]{3,2,1,0:T(2,128)(2,1)}), bf16[64,65,2,128]{3,2,1,0:T(2,128)(2,1)S(1)}, u32[]{:S(2)}, u32[]{:S(2)}) %all-to-all-start.2) | async-done | bytes 2129952 | tf_op jit(solution)/shard_map/all_to_all | solution.py:354
  151.6 2.4 %finish.1 = (bf16[64,112,128]{2,1,0:T(8,128)(2,1)}, bf16[64,16,128]{2,1,0:T(8,128)(2,1)}, f32[2,128]{1,0:T(2,128)}) custom-call(bf16[8320,128]{1,0:T(8,128)(2,1)S(1)} %bitcast.56, f32[64,2,128]{2,1,0:T(2,128)S(1)} %and_convert_fusion.choice_ref), custom_call_target="tpu_custom_call" | custom-call | tf_op jit(solution)/shard_map/finish/pallas_call | solution.py:297
  (4 shorter events, 0.0 us)
Async XLA Ops:
  0.6 28.6 %copy-start.1 = (f32[1,64,4,512]{3,2,1,0:T(4,128)S(1)}, f32[1,64,4,512]{3,2,1,0:T(4,128)}, u32[]{:S(2)}) copy-start(f32[1,64,4,512]{3,2,1,0:T(4,128)} %param.8) | copy-start | bytes 1572868
  23.4 8.3 %collective-permute-start = (f32[8,128]{1,0:T(8,128)S(1)}, f32[8,128]{1,0:T(8,128)S(1)}, u32[]{:S(2)}, u32[]{:S(2)}) collective-permute-start(f32[8,128]{1,0:T(8,128)S(1)} %row_sum.1.refs_0_), channel_id=1, source_target_pairs={{0,1},{1,2},{2,3},{3,0},{4,5},{5,6},{6,7},{7,4},{8,9},{9,10},{10,1... | collective-permute-start | bytes 12296 | tf_op jit(solution)/shard_map/ppermute | solution.py:343
  25.0 6.7 %collective-permute-start.1 = (f32[8,128]{1,0:T(8,128)S(1)}, f32[8,128]{1,0:T(8,128)S(1)}, u32[]{:S(2)}, u32[]{:S(2)}) collective-permute-start(f32[8,128]{1,0:T(8,128)S(1)} %row_sum.1.refs_0_), channel_id=1, source_target_pairs={{0,2},{1,3},{2,0},{3,1},{4,6},{5,7},{6,4},{7,5},{8,10},{9,11},{10,... | collective-permute-start | bytes 12296 | tf_op jit(solution)/shard_map/ppermute | solution.py:343
  27.9 3.8 %collective-permute-start.2 = (f32[8,128]{1,0:T(8,128)S(1)}, f32[8,128]{1,0:T(8,128)S(1)}, u32[]{:S(2)}, u32[]{:S(2)}) collective-permute-start(f32[8,128]{1,0:T(8,128)S(1)} %row_sum.1.refs_0_), channel_id=1, source_target_pairs={{0,3},{1,0},{2,1},{3,2},{4,7},{5,4},{6,5},{7,6},{8,11},{9,8},{10,9... | collective-permute-start | bytes 12296 | tf_op jit(solution)/shard_map/ppermute | solution.py:343
  29.3 2.0 %copy-start = (f32[1,64,2,7168]{3,2,1,0:T(2,128)S(1)}, f32[1,64,2,7168]{3,2,1,0:T(2,128)}, u32[]{:S(2)}) copy-start(f32[1,64,2,7168]{3,2,1,0:T(2,128)} %param.6) | copy-start | bytes 11010052
  94.2 5.5 %copy-start.2 = (s32[1,2,64,1]{2,3,1,0:T(1,128)S(1)}, s32[1,2,64,1]{2,3,1,0:T(1,128)}, u32[]{:S(2)}) copy-start(s32[1,2,64,1]{2,3,1,0:T(1,128)} %param.9) | copy-start | bytes 1540
  94.2 57.4 %all-to-all-start.2 = ((bf16[64,65,2,128]{3,2,1,0:T(2,128)(2,1)}), bf16[64,65,2,128]{3,2,1,0:T(2,128)(2,1)S(1)}, u32[]{:S(2)}, u32[]{:S(2)}) async-start(bf16[64,65,2,128]{3,2,1,0:T(2,128)(2,1)} %bitcast.61), calls=%async_computation.2 | async-start | bytes 4259840 | tf_op jit(solution)/shard_map/all_to_all | solution.py:354

commit v4 on v3

--- a/solution.py
+++ b/solution.py
@@ -33,6 +33,7 @@
 HBM = pl.BlockSpec(memory_space=pltpu.HBM)
 VMEM = pl.BlockSpec(memory_space=pltpu.VMEM)
 CHUNKS = 8
+PITCH = 136
 GRANT = 60 * 1024 * 1024
 ORTHO = 40 * 1024 * 1024
 
@@ -200,7 +201,7 @@
 
 def orthogonal_kernel(sizes, got_ref, back_hbm, wide_ref, back_ref, out_ref, val_ref, sems):
     sources, depth, _ = got_ref.shape
-    pitch, given = wide_ref.shape[0] // sources, back_ref.shape[0] // sources
+    pitch, given = PITCH, back_ref.shape[0] // sources
     matrices = [(ref, rows, columns) for ref, (rows, columns) in zip((out_ref, val_ref), sizes)]
     for s in range(sources):
         wide_ref[s * pitch : s * pitch + depth, :] = got_ref[s].astype(F32)
@@ -250,14 +251,14 @@
         copy.wait()
 
 
-def orthogonalize(got, sizes, given, pitch=136):
+def orthogonalize(got, sizes, given):
     sources = got.shape[0]
     return pl.pallas_call(
         functools.partial(orthogonal_kernel, sizes),
         in_specs=[VMEM],
         out_specs=HBM,
         out_shape=pltpu.HBM((sources * given, LANES), BF16),
-        scratch_shapes=[pltpu.VMEM((sources * pitch, LANES), F32), pltpu.VMEM((sources * given, LANES), BF16)]
+        scratch_shapes=[pltpu.VMEM(((sources + 1) * PITCH, LANES), F32), pltpu.VMEM((sources * given, LANES), BF16)]
         + [pltpu.VMEM((rows * sources, columns), BF16) for rows, columns in sizes]
         + [pltpu.SemaphoreType.DMA((CHUNKS,))],
         compiler_params=pltpu.CompilerParams(vmem_limit_bytes=ORTHO),

time: 154 us -> 154 us (level)
  no operation moved by 1% of the time
where the time goes in v4:
time: 154 us
  blocking collectives  76.5 us (50%)
  waiting for transfers between devices  44.3 us (29%)
  Pallas kernels  18.4 us (12%)
  starting transfers between devices  11.3 us (7%)
  local copies, waits for them, and re-layouts  2.26 us (1%)
    all_to_all x1, blocking collectives, body(): got = lax.all_to_all(send, 'dp', split_axis=0, concat_axis=0, tiled=True)  56.1 us
    all_to_all x1, waiting for transfers between devices, body(): lax.all_to_all(back.reshape(heads, given // 2, 2, LANES), 'dp', split_axi...  44.3 us
    all_to_all x1, blocking collectives, body(): lax.all_to_all(squares.reshape(owners, 1, LANES), 'dp', split_axis=0, con...  20.4 us
    pallas_call x1, Pallas kernels, next_momentum(): pl.pallas_call(next_kernel, grid=(steps,), in_specs=[pl.BlockSpec((8, LAN...  7.06 us
    ppermute x3, starting transfers between devices, body(): lax.ppermute(mine, 'layer', [(i, (i + shift) % layers) for i in range(lay...  5.9 us
    all_to_all x1, starting transfers between devices, body(): lax.all_to_all(back.reshape(heads, given // 2, 2, LANES), 'dp', split_axi...  5.44 us
    pallas_call x1, Pallas kernels, orthogonalize(): pl.pallas_call(functools.partial(orthogonal_kernel, sizes), in_specs=[VME...  5.06 us
  transfers between devices with their start and end apart: 4, of which 1 were waited for; matrix products, arithmetic and copies ran while one was open for 0% of the time, Pallas kernels for 5%

profile of v4, /device:TPU:2, one launch (start us, length us, event | category | flops | bytes accessed | tf_op | source)
XLA Modules:
  0.0 154.0 jit_solution(3859133350753836322)
XLA Ops:
  0.6 0.0 copy-start.1
  0.6 2.3 %squares.1 = (f32[64,128]{1,0:T(8,128)S(1)}, bf16[64,112,128]{2,1,0:T(8,128)(2,1)S(1)}, bf16[64,16,128]{2,1,0:T(8,128)(2,1)S(1)}) custom-call(bf16[64,112,128]{2,1,0:T(8,128)(2,1)} %bitcast.62, bf16[64,16,128]{2,1,0:T(8,128)(2,1)} %bitcast.64), custom_call_target="tpu_custom_call" | custom-call | tf_op jit(solution)/shard_map/squares/pallas_call | solution.py:70
  2.9 20.4 %all_to_all.15 = f32[64,1,128]{2,1,0:T(1,128)S(1)} all-to-all(f32[64,1,128]{2,1,0:T(1,128)S(1)} %bitcast.60), channel_id=1, replica_groups=mesh['dp'=64,'layer'=4] {'dp'}, dimensions={0} | all-to-all | bytes 65536 | tf_op jit(solution)/shard_map/all_to_all | solution.py:333
  23.4 1.7 %collective-permute-start = (f32[8,128]{1,0:T(8,128)S(1)}, f32[8,128]{1,0:T(8,128)S(1)}, u32[]{:S(2)}, u32[]{:S(2)}) collective-permute-start(f32[8,128]{1,0:T(8,128)S(1)} %row_sum.1.refs_0_), channel_id=1, source_target_pairs={{0,1},{1,2},{2,3},{3,0},{4,5},{5,6},{6,7},{7,4},{8,9},{9,10},{10,1... | collective-permute-start | bytes 12296 | tf_op jit(solution)/shard_map/ppermute | solution.py:344
  25.0 2.9 %collective-permute-start.1 = (f32[8,128]{1,0:T(8,128)S(1)}, f32[8,128]{1,0:T(8,128)S(1)}, u32[]{:S(2)}, u32[]{:S(2)}) collective-permute-start(f32[8,128]{1,0:T(8,128)S(1)} %row_sum.1.refs_0_), channel_id=1, source_target_pairs={{0,2},{1,3},{2,0},{3,1},{4,6},{5,7},{6,4},{7,5},{8,10},{9,11},{10,... | collective-permute-start | bytes 12296 | tf_op jit(solution)/shard_map/ppermute | solution.py:344
  27.9 1.3 collective-permute-start.2
  29.3 0.0 copy-done.1
  29.3 0.0 copy-start
  29.3 2.0 %copy-done = f32[1,64,2,7168]{3,2,1,0:T(2,128)S(1)} copy-done((f32[1,64,2,7168]{3,2,1,0:T(2,128)S(1)}, f32[1,64,2,7168]{3,2,1,0:T(2,128)}, u32[]{:S(2)}) %copy-start) | copy-done | bytes 3670040
  31.3 0.4 prepare.1.refs_6_
  31.7 0.0 collective-permute-done.refs_1_
  31.7 0.0 collective-permute-done.1.refs_2_
  31.7 0.0 collective-permute-done.2.refs_3_
  31.7 1.3 send.1
  33.0 56.1 %all_to_all.16.got_ref = bf16[64,128,128]{2,1,0:T(8,128)(2,1)S(1)} all-to-all(bf16[64,128,128]{2,1,0:T(8,128)(2,1)S(1)} %get-tuple-element.24), channel_id=1, replica_groups=mesh['dp'=64,'layer'=4] {'dp'}, dimensions={0} | all-to-all | bytes 4194304 | tf_op jit(solution)/shard_map/all_to_all | solution.py:350
  89.1 5.1 %orthogonal.1 = bf16[8320,128]{1,0:T(8,128)(2,1)} custom-call(bf16[64,128,128]{2,1,0:T(8,128)(2,1)S(1)} %all_to_all.16.got_ref), custom_call_target="tpu_custom_call" | custom-call | tf_op jit(solution)/shard_map/orthogonal/pallas_call | solution.py:256
  94.2 0.0 copy-start.2
  94.2 5.4 %all-to-all-start.2 = ((bf16[64,65,2,128]{3,2,1,0:T(2,128)(2,1)}), bf16[64,65,2,128]{3,2,1,0:T(2,128)(2,1)S(1)}, u32[]{:S(2)}, u32[]{:S(2)}) async-start(bf16[64,65,2,128]{3,2,1,0:T(2,128)(2,1)} %bitcast.61), calls=%async_computation.2 | async-start | bytes 4259840 | tf_op jit(solution)/shard_map/all_to_all | solution.py:355
  99.6 0.0 copy-done.2
  99.7 0.1 multiply_reduce_fusion
  99.8 0.1 copy.37
  99.9 0.1 copy.36
  100.0 0.2 and_convert_fusion.choice_ref
  100.2 7.1 %next.1 = (f32[64,112,128]{2,1,0:T(8,128)}, f32[64,16,128]{2,1,0:T(8,128)}) custom-call(f32[8,128]{1,0:T(8,128)} %get-tuple-element.26.clip_ref, bf16[64,112,128]{2,1,0:T(8,128)(2,1)} %bitcast.63, f32[64,112,128]{2,1,0:T(8,128)} %bitcast.54, bf16[64,16,128]{2,1,0:T(8,128)(2,1)} %bitcast.65, f32[64,16,128]{2,1,0:T(8,128)} %bitcast.57), custom_call_target="tpu_custom_call" | custom-call | tf_op jit(solution)/shard_map/next/pallas_call | solution.py:160
  107.3 44.3 %all-to-all-done.2 = bf16[64,65,2,128]{3,2,1,0:T(2,128)(2,1)S(1)} async-done(((bf16[64,65,2,128]{3,2,1,0:T(2,128)(2,1)}), bf16[64,65,2,128]{3,2,1,0:T(2,128)(2,1)S(1)}, u32[]{:S(2)}, u32[]{:S(2)}) %all-to-all-start.2) | async-done | bytes 2129952 | tf_op jit(solution)/shard_map/all_to_all | solution.py:355
  151.6 2.4 %finish.1 = (bf16[64,112,128]{2,1,0:T(8,128)(2,1)}, bf16[64,16,128]{2,1,0:T(8,128)(2,1)}, f32[2,128]{1,0:T(2,128)}) custom-call(bf16[8320,128]{1,0:T(8,128)(2,1)S(1)} %bitcast.56, f32[64,2,128]{2,1,0:T(2,128)S(1)} %and_convert_fusion.choice_ref), custom_call_target="tpu_custom_call" | custom-call | tf_op jit(solution)/shard_map/finish/pallas_call | solution.py:298
  (4 shorter events, 0.0 us)
Async XLA Ops:
  0.6 28.6 %copy-start.1 = (f32[1,64,4,512]{3,2,1,0:T(4,128)S(1)}, f32[1,64,4,512]{3,2,1,0:T(4,128)}, u32[]{:S(2)}) copy-start(f32[1,64,4,512]{3,2,1,0:T(4,128)} %param.8) | copy-start | bytes 1572868
  23.4 8.3 %collective-permute-start = (f32[8,128]{1,0:T(8,128)S(1)}, f32[8,128]{1,0:T(8,128)S(1)}, u32[]{:S(2)}, u32[]{:S(2)}) collective-permute-start(f32[8,128]{1,0:T(8,128)S(1)} %row_sum.1.refs_0_), channel_id=1, source_target_pairs={{0,1},{1,2},{2,3},{3,0},{4,5},{5,6},{6,7},{7,4},{8,9},{9,10},{10,1... | collective-permute-start | bytes 12296 | tf_op jit(solution)/shard_map/ppermute | solution.py:344
  25.0 6.7 %collective-permute-start.1 = (f32[8,128]{1,0:T(8,128)S(1)}, f32[8,128]{1,0:T(8,128)S(1)}, u32[]{:S(2)}, u32[]{:S(2)}) collective-permute-start(f32[8,128]{1,0:T(8,128)S(1)} %row_sum.1.refs_0_), channel_id=1, source_target_pairs={{0,2},{1,3},{2,0},{3,1},{4,6},{5,7},{6,4},{7,5},{8,10},{9,11},{10,... | collective-permute-start | bytes 12296 | tf_op jit(solution)/shard_map/ppermute | solution.py:344
  27.9 3.8 %collective-permute-start.2 = (f32[8,128]{1,0:T(8,128)S(1)}, f32[8,128]{1,0:T(8,128)S(1)}, u32[]{:S(2)}, u32[]{:S(2)}) collective-permute-start(f32[8,128]{1,0:T(8,128)S(1)} %row_sum.1.refs_0_), channel_id=1, source_target_pairs={{0,3},{1,0},{2,1},{3,2},{4,7},{5,4},{6,5},{7,6},{8,11},{9,8},{10,9... | collective-permute-start | bytes 12296 | tf_op jit(solution)/shard_map/ppermute | solution.py:344
  29.3 2.0 %copy-start = (f32[1,64,2,7168]{3,2,1,0:T(2,128)S(1)}, f32[1,64,2,7168]{3,2,1,0:T(2,128)}, u32[]{:S(2)}) copy-start(f32[1,64,2,7168]{3,2,1,0:T(2,128)} %param.6) | copy-start | bytes 11010052
  94.2 5.5 %copy-start.2 = (s32[1,2,64,1]{2,3,1,0:T(1,128)S(1)}, s32[1,2,64,1]{2,3,1,0:T(1,128)}, u32[]{:S(2)}) copy-start(s32[1,2,64,1]{2,3,1,0:T(1,128)} %param.9) | copy-start | bytes 1540
  94.2 57.4 %all-to-all-start.2 = ((bf16[64,65,2,128]{3,2,1,0:T(2,128)(2,1)}), bf16[64,65,2,128]{3,2,1,0:T(2,128)(2,1)S(1)}, u32[]{:S(2)}, u32[]{:S(2)}) async-start(bf16[64,65,2,128]{3,2,1,0:T(2,128)(2,1)} %bitcast.61), calls=%async_computation.2 | async-start | bytes 4259840 | tf_op jit(solution)/shard_map/all_to_all | solution.py:355

commit v5 on v4

--- a/solution.py
+++ b/solution.py
@@ -341,7 +341,7 @@
     mine, *momenta = lax.optimization_barrier((mine, out_momentum, val_momentum))
     decayed = prepare(*momenta)
     parts = [mine] + [
-        lax.ppermute(mine, "layer", [(i, (i + shift) % layers) for i in range(layers)]) for shift in range(1, layers)
+        lax.ppermute(mine, "layer", [(i, (i + shift) % layers) for i in range(layers)]) for shift in sorted(range(1, layers), key=lambda d: -min(d, layers - d))
     ]
     count = (output_grad.size + values_grad.size) * everyone
 

time: 154 us -> 155 us (level)
  no operation moved by 1% of the time
where the time goes in v5:
time: 155 us
  blocking collectives  76.5 us (49%)
  waiting for transfers between devices  44.3 us (29%)
  Pallas kernels  18.4 us (12%)
  starting transfers between devices  12 us (8%)
  local copies, waits for them, and re-layouts  2.26 us (1%)
    all_to_all x1, blocking collectives, body(): got = lax.all_to_all(send, 'dp', split_axis=0, concat_axis=0, tiled=True)  56.1 us
    all_to_all x1, waiting for transfers between devices, body(): lax.all_to_all(back.reshape(heads, given // 2, 2, LANES), 'dp', split_axi...  44.3 us
    all_to_all x1, blocking collectives, body(): lax.all_to_all(squares.reshape(owners, 1, LANES), 'dp', split_axis=0, con...  20.4 us
    pallas_call x1, Pallas kernels, next_momentum(): pl.pallas_call(next_kernel, grid=(steps,), in_specs=[pl.BlockSpec((8, LAN...  7.06 us
    ppermute x3, starting transfers between devices, body(): lax.ppermute(mine, 'layer', [(i, (i + shift) % layers) for i in range(lay...  6.51 us
    all_to_all x1, starting transfers between devices, body(): lax.all_to_all(back.reshape(heads, given // 2, 2, LANES), 'dp', split_axi...  5.44 us
    pallas_call x1, Pallas kernels, orthogonalize(): pl.pallas_call(functools.partial(orthogonal_kernel, sizes), in_specs=[VME...  5.06 us
  transfers between devices with their start and end apart: 4, of which 1 were waited for; matrix products, arithmetic and copies ran while one was open for 0% of the time, Pallas kernels for 5%

profile of v5, /device:TPU:2, one launch (start us, length us, event | category | flops | bytes accessed | tf_op | source)
XLA Modules:
  0.0 154.6 jit_solution(2618503487129395971)
XLA Ops:
  0.6 0.0 copy-start.1
  0.6 2.3 %squares.1 = (f32[64,128]{1,0:T(8,128)S(1)}, bf16[64,112,128]{2,1,0:T(8,128)(2,1)S(1)}, bf16[64,16,128]{2,1,0:T(8,128)(2,1)S(1)}) custom-call(bf16[64,112,128]{2,1,0:T(8,128)(2,1)} %bitcast.62, bf16[64,16,128]{2,1,0:T(8,128)(2,1)} %bitcast.64), custom_call_target="tpu_custom_call" | custom-call | tf_op jit(solution)/shard_map/squares/pallas_call | solution.py:70
  2.9 20.4 %all_to_all.15 = f32[64,1,128]{2,1,0:T(1,128)S(1)} all-to-all(f32[64,1,128]{2,1,0:T(1,128)S(1)} %bitcast.60), channel_id=1, replica_groups=mesh['dp'=64,'layer'=4] {'dp'}, dimensions={0} | all-to-all | bytes 65536 | tf_op jit(solution)/shard_map/all_to_all | solution.py:333
  23.4 3.3 %collective-permute-start = (f32[8,128]{1,0:T(8,128)S(1)}, f32[8,128]{1,0:T(8,128)S(1)}, u32[]{:S(2)}, u32[]{:S(2)}) collective-permute-start(f32[8,128]{1,0:T(8,128)S(1)} %row_sum.1.refs_0_), channel_id=1, source_target_pairs={{0,2},{1,3},{2,0},{3,1},{4,6},{5,7},{6,4},{7,5},{8,10},{9,11},{10,... | collective-permute-start | bytes 12296 | tf_op jit(solution)/shard_map/ppermute | solution.py:344
  26.6 0.7 collective-permute-start.1
  27.3 2.6 %collective-permute-start.2 = (f32[8,128]{1,0:T(8,128)S(1)}, f32[8,128]{1,0:T(8,128)S(1)}, u32[]{:S(2)}, u32[]{:S(2)}) collective-permute-start(f32[8,128]{1,0:T(8,128)S(1)} %row_sum.1.refs_0_), channel_id=1, source_target_pairs={{0,3},{1,0},{2,1},{3,2},{4,7},{5,4},{6,5},{7,6},{8,11},{9,8},{10,9... | collective-permute-start | bytes 12296 | tf_op jit(solution)/shard_map/ppermute | solution.py:344
  29.9 0.0 copy-done.1
  29.9 0.0 copy-start
  29.9 2.0 %copy-done = f32[1,64,2,7168]{3,2,1,0:T(2,128)S(1)} copy-done((f32[1,64,2,7168]{3,2,1,0:T(2,128)S(1)}, f32[1,64,2,7168]{3,2,1,0:T(2,128)}, u32[]{:S(2)}) %copy-start) | copy-done | bytes 3670040
  31.9 0.4 prepare.1.refs_6_
  32.3 0.0 collective-permute-done.refs_1_
  32.3 0.0 collective-permute-done.1.refs_2_
  32.3 0.0 collective-permute-done.2.refs_3_
  32.3 1.3 send.1
  33.6 56.1 %all_to_all.16.got_ref = bf16[64,128,128]{2,1,0:T(8,128)(2,1)S(1)} all-to-all(bf16[64,128,128]{2,1,0:T(8,128)(2,1)S(1)} %get-tuple-element.24), channel_id=1, replica_groups=mesh['dp'=64,'layer'=4] {'dp'}, dimensions={0} | all-to-all | bytes 4194304 | tf_op jit(solution)/shard_map/all_to_all | solution.py:350
  89.7 5.1 %orthogonal.1 = bf16[8320,128]{1,0:T(8,128)(2,1)} custom-call(bf16[64,128,128]{2,1,0:T(8,128)(2,1)S(1)} %all_to_all.16.got_ref), custom_call_target="tpu_custom_call" | custom-call | tf_op jit(solution)/shard_map/orthogonal/pallas_call | solution.py:256
  94.8 0.0 copy-start.2
  94.8 5.4 %all-to-all-start.2 = ((bf16[64,65,2,128]{3,2,1,0:T(2,128)(2,1)}), bf16[64,65,2,128]{3,2,1,0:T(2,128)(2,1)S(1)}, u32[]{:S(2)}, u32[]{:S(2)}) async-start(bf16[64,65,2,128]{3,2,1,0:T(2,128)(2,1)} %bitcast.61), calls=%async_computation.2 | async-start | bytes 4259840 | tf_op jit(solution)/shard_map/all_to_all | solution.py:355
  100.2 0.0 copy-done.2
  100.3 0.1 multiply_reduce_fusion
  100.4 0.1 copy.37
  100.5 0.1 copy.36
  100.6 0.2 and_convert_fusion.choice_ref
  100.8 7.1 %next.1 = (f32[64,112,128]{2,1,0:T(8,128)}, f32[64,16,128]{2,1,0:T(8,128)}) custom-call(f32[8,128]{1,0:T(8,128)} %get-tuple-element.26.clip_ref, bf16[64,112,128]{2,1,0:T(8,128)(2,1)} %bitcast.63, f32[64,112,128]{2,1,0:T(8,128)} %bitcast.54, bf16[64,16,128]{2,1,0:T(8,128)(2,1)} %bitcast.65, f32[64,16,128]{2,1,0:T(8,128)} %bitcast.57), custom_call_target="tpu_custom_call" | custom-call | tf_op jit(solution)/shard_map/next/pallas_call | solution.py:160
  107.9 44.3 %all-to-all-done.2 = bf16[64,65,2,128]{3,2,1,0:T(2,128)(2,1)S(1)} async-done(((bf16[64,65,2,128]{3,2,1,0:T(2,128)(2,1)}), bf16[64,65,2,128]{3,2,1,0:T(2,128)(2,1)S(1)}, u32[]{:S(2)}, u32[]{:S(2)}) %all-to-all-start.2) | async-done | bytes 2129952 | tf_op jit(solution)/shard_map/all_to_all | solution.py:355
  152.2 2.4 %finish.1 = (bf16[64,112,128]{2,1,0:T(8,128)(2,1)}, bf16[64,16,128]{2,1,0:T(8,128)(2,1)}, f32[2,128]{1,0:T(2,128)}) custom-call(bf16[8320,128]{1,0:T(8,128)(2,1)S(1)} %bitcast.56, f32[64,2,128]{2,1,0:T(2,128)S(1)} %and_convert_fusion.choice_ref), custom_call_target="tpu_custom_call" | custom-call | tf_op jit(solution)/shard_map/finish/pallas_call | solution.py:298
  (4 shorter events, 0.0 us)
Async XLA Ops:
  0.6 29.2 %copy-start.1 = (f32[1,64,4,512]{3,2,1,0:T(4,128)S(1)}, f32[1,64,4,512]{3,2,1,0:T(4,128)}, u32[]{:S(2)}) copy-start(f32[1,64,4,512]{3,2,1,0:T(4,128)} %param.8) | copy-start | bytes 1572868
  23.4 8.9 %collective-permute-start = (f32[8,128]{1,0:T(8,128)S(1)}, f32[8,128]{1,0:T(8,128)S(1)}, u32[]{:S(2)}, u32[]{:S(2)}) collective-permute-start(f32[8,128]{1,0:T(8,128)S(1)} %row_sum.1.refs_0_), channel_id=1, source_target_pairs={{0,2},{1,3},{2,0},{3,1},{4,6},{5,7},{6,4},{7,5},{8,10},{9,11},{10,... | collective-permute-start | bytes 12296 | tf_op jit(solution)/shard_map/ppermute | solution.py:344
  26.6 5.7 %collective-permute-start.1 = (f32[8,128]{1,0:T(8,128)S(1)}, f32[8,128]{1,0:T(8,128)S(1)}, u32[]{:S(2)}, u32[]{:S(2)}) collective-permute-start(f32[8,128]{1,0:T(8,128)S(1)} %row_sum.1.refs_0_), channel_id=1, source_target_pairs={{0,1},{1,2},{2,3},{3,0},{4,5},{5,6},{6,7},{7,4},{8,9},{9,10},{10,1... | collective-permute-start | bytes 12296 | tf_op jit(solution)/shard_map/ppermute | solution.py:344
  27.3 5.0 %collective-permute-start.2 = (f32[8,128]{1,0:T(8,128)S(1)}, f32[8,128]{1,0:T(8,128)S(1)}, u32[]{:S(2)}, u32[]{:S(2)}) collective-permute-start(f32[8,128]{1,0:T(8,128)S(1)} %row_sum.1.refs_0_), channel_id=1, source_target_pairs={{0,3},{1,0},{2,1},{3,2},{4,7},{5,4},{6,5},{7,6},{8,11},{9,8},{10,9... | collective-permute-start | bytes 12296 | tf_op jit(solution)/shard_map/ppermute | solution.py:344
  29.9 2.0 %copy-start = (f32[1,64,2,7168]{3,2,1,0:T(2,128)S(1)}, f32[1,64,2,7168]{3,2,1,0:T(2,128)}, u32[]{:S(2)}) copy-start(f32[1,64,2,7168]{3,2,1,0:T(2,128)} %param.6) | copy-start | bytes 11010052
  94.8 5.5 %copy-start.2 = (s32[1,2,64,1]{2,3,1,0:T(1,128)S(1)}, s32[1,2,64,1]{2,3,1,0:T(1,128)}, u32[]{:S(2)}) copy-start(s32[1,2,64,1]{2,3,1,0:T(1,128)} %param.9) | copy-start | bytes 1540
  94.8 57.4 %all-to-all-start.2 = ((bf16[64,65,2,128]{3,2,1,0:T(2,128)(2,1)}), bf16[64,65,2,128]{3,2,1,0:T(2,128)(2,1)S(1)}, u32[]{:S(2)}, u32[]{:S(2)}) async-start(bf16[64,65,2,128]{3,2,1,0:T(2,128)(2,1)} %bitcast.61), calls=%async_computation.2 | async-start | bytes 4259840 | tf_op jit(solution)/shard_map/all_to_all | solution.py:355
